TPU v7x, 512 devices: a whole 4x4x16 slice. The times are simulated.
512 devices in a mesh: dp: 32 (over z, core), ctx: 16 (over x, y).
Axes of the slice: x: 4, y: 4, z: 16, core: 2. Of those that a mesh axis runs over, the one named last changes fastest.
Arguments:
- queries: bfloat16 [32, 2048, 2048], P('dp', 'ctx'), may hold values from -6 to 6
- key_vectors: bfloat16 [32, 2048, 2048], P('dp', 'ctx'), may hold values from -6 to 6
- values: bfloat16 [32, 2048, 2048], P('dp', 'ctx'), may hold values from -60 to 60
- grad_out: bfloat16 [32, 2048, 2048], P('dp', 'ctx'), may hold values from -40 to 40
- log_decay: float32 [32, 8, 2048], P('dp', None, 'ctx'), may hold values from -1 to 0, as said below
- norm_gain: float32 [2048], replicated, may hold values from 0.1 to 1.9
Outputs:
- grad_queries: bfloat16 [32, 2048, 2048], P('dp', 'ctx')
- grad_keys: bfloat16 [32, 2048, 2048], P('dp', 'ctx')
- grad_values: bfloat16 [32, 2048, 2048], P('dp', 'ctx')
- grad_gain: float32 [2048], replicated
Inputs may be any that keep to these rules, and one draw needn't show every extreme that they name: log_decay is never positive.
All inputs are finite; a program needn't handle non-finite values.
Results may differ from a plain program's by a relative error of at most 0.029.
Values may be sent and summed in bfloat16 or wider, within the bound.
No kernel may reach another device: no remote copies, remote signals or barrier semaphores. Data moves between devices by JAX's collectives and lax.ppermute only.
A program may use at most 64 MiB of HBM per device.

v0:
```python
import jax
import jax.numpy as jnp
from jax import lax
from jax.sharding import PartitionSpec as P

HEADS = 8
KD = 256
VD = 256


EPSILON = 1e-05


def prefix(value, axis, combine, identity, reverse):
    length, place = (lax.axis_size(axis), lax.axis_index(axis))
    everything = jax.tree.map(lambda part: lax.all_gather(part, axis), value)
    start = jax.tree.map(
        lambda part, zero: jnp.broadcast_to(jnp.asarray(zero, part.dtype), part.shape),
        value,
        identity,
    )

    def turn(k, before):
        at = length - 1 - k if reverse else k
        reached = at > place if reverse else at < place
        new = combine(before, jax.tree.map(lambda part: part[at], everything))
        return jax.tree.map(lambda a, b: jnp.where(reached, a, b), new, before)

    return lax.fori_loop(0, length, turn, start)


def combine(earlier, later):
    later_total = later[0].astype(jnp.float32)
    summed = (earlier[0].astype(jnp.float32) + later_total).astype(jnp.bfloat16)
    carried = (
        jnp.exp(later_total)[..., None, None] * earlier[1].astype(jnp.float32)
        + later[1].astype(jnp.float32)
    ).astype(jnp.bfloat16)
    return (summed, carried)


def head_grads(query_heads, key_heads, value_heads, out_heads, decay, gain_heads):
    row_count = query_heads.shape[1]
    scaling = query_heads.shape[3] ** (-0.5)
    cumulative = jnp.cumsum(decay, axis=2)
    block_end = cumulative[:, :, -1]
    position = jnp.arange(row_count)
    causal = position[:, None] >= position[None, :]
    weight = jnp.where(
        causal, jnp.exp(jnp.minimum(cumulative[..., :, None] - cumulative[..., None, :], 0.0)), 0.0
    )
    scores = jnp.einsum(
        "bthk,bshk->bhts", query_heads, key_heads, preferred_element_type=jnp.float32
    )
    retained = (scores * scaling * weight).astype(jnp.bfloat16)
    to_end = jnp.exp(block_end[:, :, None] - cumulative).transpose(0, 2, 1)[..., None]
    key_tail = (key_heads.astype(jnp.float32) * to_end).astype(jnp.bfloat16)
    block_state = jnp.einsum(
        "bshk,bshv->bhkv", key_tail, value_heads, preferred_element_type=jnp.float32
    ).astype(jnp.bfloat16)
    block_total = block_end.astype(jnp.bfloat16)
    identity = (jnp.zeros_like(block_total), jnp.zeros_like(block_state))
    _, state_in = prefix((block_total, block_state), "ctx", combine, identity, False)
    from_start = (scaling * jnp.exp(cumulative)).transpose(0, 2, 1)[..., None]
    query_tail = (query_heads.astype(jnp.float32) * from_start).astype(jnp.bfloat16)
    output = jnp.einsum(
        "bhts,bshv->bthv", retained, value_heads, preferred_element_type=jnp.float32
    )
    output = output + jnp.einsum(
        "bthk,bhkv->bthv", query_tail, state_in, preferred_element_type=jnp.float32
    )
    centred = output - jnp.mean(output, axis=-1, keepdims=True)
    inverse = lax.rsqrt(jnp.mean(centred * centred, axis=-1, keepdims=True) + EPSILON)
    normed = centred * inverse
    out_wide = out_heads.astype(jnp.float32)
    gain_part = jnp.sum(out_wide * normed, axis=(0, 1))
    scaled_grad = out_wide * gain_heads
    grad_o = inverse * (
        scaled_grad
        - jnp.mean(scaled_grad, axis=-1, keepdims=True)
        - normed * jnp.mean(scaled_grad * normed, axis=-1, keepdims=True)
    )
    grad_o = grad_o.astype(jnp.bfloat16)
    grad_scores = jnp.einsum(
        "bthv,bshv->bhts", grad_o, value_heads, preferred_element_type=jnp.float32
    )
    grad_retained = (grad_scores * scaling * weight).astype(jnp.bfloat16)
    local_queries = jnp.einsum(
        "bhts,bshk->bthk", grad_retained, key_heads, preferred_element_type=jnp.float32
    )
    local_keys = jnp.einsum(
        "bhts,bthk->bshk", grad_retained, query_heads, preferred_element_type=jnp.float32
    )
    local_values = jnp.einsum(
        "bhts,bthv->bshv", retained, grad_o, preferred_element_type=jnp.float32
    )
    block_grad = jnp.einsum(
        "bthk,bthv->bhkv", query_tail, grad_o, preferred_element_type=jnp.float32
    ).astype(jnp.bfloat16)
    _, grad_in = prefix((block_total, block_grad), "ctx", combine, identity, True)
    cross_queries = (
        jnp.einsum("bthv,bhkv->bthk", grad_o, state_in, preferred_element_type=jnp.float32)
        * from_start
    )
    cross_keys = (
        jnp.einsum("bshv,bhkv->bshk", value_heads, grad_in, preferred_element_type=jnp.float32)
        * to_end
    )
    cross_values = (
        jnp.einsum("bshk,bhkv->bshv", key_heads, grad_in, preferred_element_type=jnp.float32)
        * to_end
    )
    grad_queries = (local_queries + cross_queries).astype(jnp.bfloat16)
    grad_keys = (local_keys + cross_keys).astype(jnp.bfloat16)
    grad_values = (local_values + cross_values).astype(jnp.bfloat16)
    return (grad_queries, grad_keys, grad_values, gain_part)


def shards(queries, key_vectors, values, grad_out, log_decay, norm_gain):
    seq_count, row_count = (queries.shape[0], queries.shape[1])
    query_heads = queries.reshape(seq_count, row_count, HEADS, KD)
    key_heads = key_vectors.reshape(seq_count, row_count, HEADS, KD)
    value_heads = values.reshape(seq_count, row_count, HEADS, VD)
    out_heads = grad_out.reshape(seq_count, row_count, HEADS, VD)
    gain_heads = norm_gain.reshape(HEADS, VD)
    head_ranges = [(0, HEADS)]
    results = [
        head_grads(query_heads, key_heads, value_heads, out_heads, log_decay, gain_heads)
        for first_head, end_head in head_ranges
    ]
    grad_queries = jnp.concatenate([item[0] for item in results], axis=2).reshape(
        seq_count, row_count, HEADS * KD
    )
    grad_keys = jnp.concatenate([item[1] for item in results], axis=2).reshape(
        seq_count, row_count, HEADS * KD
    )
    grad_values = jnp.concatenate([item[2] for item in results], axis=2).reshape(
        seq_count, row_count, HEADS * VD
    )
    gain_part = jnp.concatenate([item[3] for item in results], axis=0)
    gain_sum = lax.psum(gain_part, ("dp", "ctx"))
    grad_gain = (gain_sum / (seq_count * lax.axis_size("dp"))).reshape(HEADS * VD)
    return (grad_queries, grad_keys, grad_values, grad_gain)


def solution(mesh):
    return jax.shard_map(
        shards,
        mesh=mesh,
        in_specs=(
            P("dp", "ctx", None),
            P("dp", "ctx", None),
            P("dp", "ctx", None),
            P("dp", "ctx", None),
            P("dp", None, "ctx"),
            P(),
        ),
        out_specs=(P("dp", "ctx", None), P("dp", "ctx", None), P("dp", "ctx", None), P()),
        check_vma=False,
    )
```

profile of v0, /device:TPU:1, one launch (start us, length us, event | category | flops | bytes accessed | tf_op | source)
XLA Modules:
  0.0 350.8 jit_solution(11499558164839564813)
XLA Ops:
  7.2 1.3 copy.155
  8.6 1.4 copy.156
  10.4 1.4 convolution_convert_fusion.1
  12.3 17.3 %all-gather = bf16[16,8,1]{1,2,0:T(2,128)(2,1)S(1)} all-gather(bf16[1,8,1]{1,2,0:T(2,128)(2,1)S(1)} %convert_element_type.199), channel_id=2, replica_groups=mesh['dp'=32,'ctx'=16] {'ctx'}, dimensions={0}, use_global_device_ids=true | all-gather | bytes 272 | tf_op jit(solution)/shard_map/all_gather | solution.py:16
  30.8 1.2 copy.121
  32.1 1.5 fusion.16
  33.6 1.3 convolution_bitcast_fusion.3
  34.9 109.1 %all-gather.6.cloned.1.call-done = bf16[128,256,256]{2,1,0:T(8,128)(2,1)} async-done(((bf16[8,256,256]{2,1,0:T(8,128)(2,1)}), bf16[128,256,256]{2,1,0:T(8,128)(2,1)}) %all-gather.6.cloned.1.call-update) | async-done | bytes 16777232 | tf_op jit(solution)/shard_map/all_gather | solution.py:16
  144.0 30.5 %while.30 = (s32[]{:T(128)}, bf16[1,8,256,256]{3,2,1,0:T(8,128)(2,1)S(1)}, s32[]{:T(128)}, bf16[16,1,8]{2,1,0:T(2,128)(2,1)S(1)}, bf16[16,1,8,256,256]{4,3,2,1,0:T(8,128)(2,1)}, /*index=5*/s32[]{:T(128)}, s32[]{:T(128)}) while((s32[]{:T(128)}, bf16[1,8,256,256]{3,2,1,0:T(8,128)(2,1)S(1)}, s32[]{:T(128)}, ...), condition=%wide.region_2.3_spmd.clone, body=%wide.region_1.2_spmd.clone.sunk | while | flops 3670028 | bytes 3145921 | solution.py:29
  144.0 1.9 fusion.44
  145.9 1.9 fusion.44
  147.8 1.9 fusion.44
  149.7 1.9 fusion.44
  151.6 1.9 fusion.44
  153.5 1.9 fusion.44
  155.4 1.9 fusion.44
  157.3 1.9 fusion.44
  159.2 1.9 fusion.44
  161.2 1.9 fusion.44
  163.1 1.9 fusion.44
  165.0 1.9 fusion.44
  166.9 1.9 fusion.44
  168.8 1.9 fusion.44
  170.7 1.9 fusion.44
  172.6 1.9 fusion.44
  174.5 1.7 fusion.28
  178.0 1.4 convolution_convert_fusion
  182.1 104.9 %psum.7 = f32[8,256]{1,0:T(8,128)S(1)} all-reduce(f32[8,256]{1,0:T(8,128)S(1)} %get-tuple-element.320), channel_id=1, replica_groups=mesh['dp'=32,'ctx'=16] {'dp','ctx'}, use_global_device_ids=true, to_apply=%region_10.11 | all-reduce | flops 2048 | bytes 16384 | tf_op jit(solution)/shard_map/psum | solution.py:141
  288.0 19.0 %all-gather.8.cloned.1.call-done = bf16[128,256,256]{2,1,0:T(8,128)(2,1)} async-done(((bf16[8,256,256]{2,1,0:T(8,128)(2,1)}), bf16[128,256,256]{2,1,0:T(8,128)(2,1)}) %all-gather.8.cloned.1.call-update) | async-done | bytes 16777232 | tf_op jit(solution)/shard_map/all_gather | solution.py:16
  307.0 30.6 %while.31 = (s32[]{:T(128)}, bf16[1,8,256,256]{3,2,1,0:T(8,128)(2,1)S(1)}, s32[]{:T(128)}, bf16[16,1,8]{2,1,0:T(2,128)(2,1)S(1)}, bf16[16,1,8,256,256]{4,3,2,1,0...) while((s32[]{:T(128)}, bf16[1,8,256,256]{3,2,1,0:T(8,128)(2,1)S(1)}, s32[]{:T(128)}, ...), condition=%wide.region_8.9_spmd.clone, body=%wide.region_7.8_spmd.clone.sunk | while | flops 3670032 | bytes 3145983 | solution.py:29
  307.0 1.9 fusion.45
  308.9 1.9 fusion.45
  310.8 1.9 fusion.45
  312.7 1.9 fusion.45
  314.6 1.9 fusion.45
  316.6 1.9 fusion.45
  318.5 1.9 fusion.45
  320.4 1.9 fusion.45
  322.3 1.9 fusion.45
  324.2 1.9 fusion.45
  326.2 1.9 fusion.45
  328.1 1.9 fusion.45
  330.0 1.9 fusion.45
  331.9 1.9 fusion.45
  333.8 1.9 fusion.45
  335.7 1.9 fusion.45
  338.7 1.1 fusion.11
  339.9 1.3 copy.132
  (92 shorter events, 11.6 us)
Async XLA Ops:
  7.2 2.8 copy-start.11
  7.2 136.8 %all-gather.6.cloned.1.call-start = ((), (), s32[]{:S(2)}) async-start(), calls=%async_computation | async-start | bytes 17825792 | tf_op jit(solution)/shard_map/all_gather | solution.py:16
  8.5 3.4 copy-start.3
  8.5 3.4 copy-start.8
  10.4 19.3 %copy-start.9 = (bf16[1,128,2048]{2,1,0:T(8,128)(2,1)S(1)}, bf16[1,128,2048]{2,1,0:T(8,128)(2,1)}, u32[]{:S(2)}) copy-start(bf16[1,128,2048]{2,1,0:T(8,128)(2,1)} %param.13) | copy-start | bytes 1572868
  11.9 20.1 %copy-start.10 = (f32[2048]{0:T(1024)S(1)}, f32[2048]{0:T(1024)}, u32[]{:S(2)}) copy-start(f32[2048]{0:T(1024)} %param.15) | copy-start | bytes 24580
  11.9 295.1 %all-gather.8.cloned.1.call-start = ((), (), s32[]{:S(2)}) async-start(), calls=%async_computation.1 | async-start | bytes 17825792 | tf_op jit(solution)/shard_map/all_gather | solution.py:16
  12.3 162.2 %copy-start = (bf16[1,128,2048]{1,2,0:T(8,128)(2,1)}, bf16[1,128,2048]{1,2,0:T(8,128)(2,1)S(1)}, u32[]{:S(2)}) copy-start(bf16[1,128,2048]{1,2,0:T(8,128)(2,1)S(1)} %copy.154) | copy-start | bytes 1572868
  176.6 1.5 copy-start.1
  179.5 1.0 copy-start.4
  179.8 0.7 copy-start.6
  337.6 1.0 copy-start.2
  337.6 1.1 copy-start.7
  338.7 3.5 copy-start.5
Sparse Core Ops, SparseCore 0:
  12.0 131.8 all-gather.5
  179.6 127.3 all-gather.7
where the time goes:
time: 353 us; the launch traced here: 351 us
  waiting for transfers between devices  128 us (36%)
  blocking collectives  122 us (35%)
  other arithmetic  62.2 us (18%)
  between operations  14.4 us (4%)
  local copies, waits for them, and re-layouts  11.9 us (3%)
  matrix products  10.7 us (3%)
    all_gather x2, waiting for transfers between devices, prefix(): everything = jax.tree.map(lambda part: lax.all_gather(part, axis), value)  128 us
    psum x1, blocking collectives, shards(): gain_sum = lax.psum(gain_part, ('dp', 'ctx'))  105 us
    select_n x32, other arithmetic, turn(): return jax.tree.map(lambda a, b: jnp.where(reached, a, b), new, before)  59.7 us
    all_gather x1, blocking collectives, prefix(): everything = jax.tree.map(lambda part: lax.all_gather(part, axis), value)  17.3 us
  transfers between devices with their start and end apart: 2, of which 2 were waited for; matrix products, arithmetic and copies ran while one was open for 3% of the time, Pallas kernels for 0%

commit v1 on v0

v1 whole, which is shorter than its diff:
```python
import functools

import jax
import jax.numpy as jnp
from jax import lax
from jax.experimental import pallas as pl
from jax.experimental.pallas import tpu as pltpu
from jax.sharding import PartitionSpec as P

HEADS = 8
KD = 256
VD = 256
EPSILON = 1e-05

TOK = 128
GROUP = 8
CHUNK = 256
CHUNKS = GROUP * TOK // CHUNK
ROWS = 4 * TOK + 16
BACK = 3 * TOK

F32 = jnp.float32
BF16 = jnp.bfloat16
SCALE = KD ** (-0.5)


def nn(a, b):
    return lax.dot_general(a, b, (((1,), (0,)), ((), ())), preferred_element_type=F32)


def nt(a, b):
    return lax.dot_general(a, b, (((1,), (1,)), ((), ())), preferred_element_type=F32)


def tn(a, b):
    return lax.dot_general(a, b, (((0,), (0,)), ((), ())), preferred_element_type=F32)


def call(kernel, outs, scratch=(), smem=()):
    def run(*args):
        specs = [
            pl.BlockSpec(memory_space=pltpu.SMEM if i in smem else pltpu.VMEM)
            for i in range(len(args))
        ]
        return pl.pallas_call(
            kernel,
            out_shape=[jax.ShapeDtypeStruct(shape, kind) for shape, kind in outs],
            in_specs=specs,
            out_specs=[pl.BlockSpec(memory_space=pltpu.VMEM) for _ in outs],
            scratch_shapes=list(scratch),
            compiler_params=pltpu.CompilerParams(vmem_limit_bytes=24 * 1024 * 1024),
        )(*args)

    return run


def pack_kernel(q_ref, k_ref, v_ref, g_ref, decay_ref, out_ref):
    row = lax.broadcasted_iota(jnp.int32, (16, 256), 0)
    for h in range(HEADS):
        cols = slice(h * KD, (h + 1) * KD)
        for n, ref in enumerate((q_ref, k_ref, v_ref, g_ref)):
            out_ref[h, n * TOK : (n + 1) * TOK, :] = ref[:, cols]
        decay = decay_ref[h : h + 1, :]
        high = decay.astype(BF16).astype(F32)
        rest = decay - high
        middle = rest.astype(BF16).astype(F32)
        low = rest - middle
        first = jnp.concatenate([high, middle], axis=1)
        second = jnp.concatenate([low, jnp.zeros_like(low)], axis=1)
        pieces = jnp.where(row == 0, first, jnp.where(row == 1, second, 0.0))
        out_ref[h, 4 * TOK :, :] = pieces.astype(BF16)


def part(ref, c, n):
    per = CHUNK // TOK
    return ref[c * per : (c + 1) * per, n * TOK : (n + 1) * TOK, :].reshape(CHUNK, 256)


def chunk_decay(col_ref, row_ref, c):
    column = col_ref[:, c : c + 1]
    line = row_ref[c : c + 1, :]
    return column, line, line[:, CHUNK - 1 :]


def chunk_weight(column, line):
    t = lax.broadcasted_iota(jnp.int32, (CHUNK, CHUNK), 0)
    s = lax.broadcasted_iota(jnp.int32, (CHUNK, CHUNK), 1)
    return jnp.where(t >= s, jnp.exp(jnp.minimum(column - line, 0.0)), 0.0)


def state_kernel(got_ref, total_ref, states_ref, col_ref, row_ref, decay_ref):
    decay_ref[...] = jnp.zeros_like(decay_ref)
    for i in range(GROUP):
        pieces = got_ref[i, 4 * TOK :, :].astype(F32)
        decay = pieces[0:1, :TOK] + pieces[0:1, TOK:] + pieces[1:2, :TOK]
        c, j = divmod(i * TOK, CHUNK)
        decay_ref[c : c + 1, j : j + TOK] = decay
    decay = decay_ref[...]
    t = lax.broadcasted_iota(jnp.int32, (CHUNK, CHUNK), 0)
    s = lax.broadcasted_iota(jnp.int32, (CHUNK, CHUNK), 1)
    lower = (t >= s).astype(F32)
    exact = dict(precision=lax.Precision.HIGHEST, preferred_element_type=F32)
    row_ref[...] = lax.dot_general(decay, lower, (((1,), (1,)), ((), ())), **exact)
    col_ref[...] = lax.dot_general(lower, decay, (((1,), (1,)), ((), ())), **exact)
    carried = jnp.zeros((KD, VD), F32)
    for c in range(CHUNKS):
        states_ref[c] = carried
        column, line, last = chunk_decay(col_ref, row_ref, c)
        key_tail = (part(got_ref, c, 1).astype(F32) * jnp.exp(last - column)).astype(BF16)
        carried = jnp.exp(last) * carried + tn(key_tail, part(got_ref, c, 2))
    total_ref[...] = carried.astype(BF16)


def local_kernel(got_ref, states_ref, col_ref, row_ref, retained_ref, output_ref):
    for c in range(CHUNKS):
        column, line, last = chunk_decay(col_ref, row_ref, c)
        q = part(got_ref, c, 0)
        scores = nt(q, part(got_ref, c, 1))
        retained = (scores * (SCALE * chunk_weight(column, line))).astype(BF16)
        retained_ref[c] = retained
        output = nn(retained, part(got_ref, c, 2))
        if c:
            tail = (q.astype(F32) * (SCALE * jnp.exp(column))).astype(BF16)
            output = output + nn(tail, states_ref[c].astype(BF16))
        output_ref[c] = output


def output_kernel(
    half_ref, got_ref, states_ref, output_ref, middle_ref, col_ref, row_ref, gain_ref,
    grad_ref, state_in_ref, state_grads_ref, total_ref, gain_part_ref, block_grads,
):
    gain = gain_ref[0:1, :]
    middle = jnp.where(half_ref[0] > 0, middle_ref[...].astype(F32), 0.0)
    middle_low = middle.astype(BF16)
    before = jnp.zeros((1, 1), F32)
    gain_part = jnp.zeros((1, VD), F32)
    for c in range(CHUNKS):
        column, line, last = chunk_decay(col_ref, row_ref, c)
        q = part(got_ref, c, 0).astype(F32)
        tail = (q * (SCALE * jnp.exp(column))).astype(BF16)
        state_in_ref[c] = (states_ref[c] + jnp.exp(before) * middle).astype(BF16)
        output = output_ref[c] + jnp.exp(before) * nn(tail, middle_low)
        before = before + last
        centred = output - jnp.mean(output, axis=1, keepdims=True)
        inverse = lax.rsqrt(jnp.mean(centred * centred, axis=1, keepdims=True) + EPSILON)
        normed = centred * inverse
        wide = part(got_ref, c, 3).astype(F32)
        gain_part = gain_part + jnp.sum(wide * normed, axis=0, keepdims=True)
        scaled = wide * gain
        grad = inverse * (
            scaled
            - jnp.mean(scaled, axis=1, keepdims=True)
            - normed * jnp.mean(scaled * normed, axis=1, keepdims=True)
        )
        grad = grad.astype(BF16)
        grad_ref[c] = grad
        block_grads[c] = tn(tail, grad)
    carried = jnp.zeros((KD, VD), F32)
    for c in reversed(range(CHUNKS)):
        state_grads_ref[c] = carried.astype(BF16)
        _, _, last = chunk_decay(col_ref, row_ref, c)
        carried = jnp.exp(last) * carried + block_grads[c]
    total_ref[...] = carried.astype(BF16)
    first = lax.broadcasted_iota(jnp.int32, (8, VD), 0) == 0
    gain_part_ref[...] = jnp.where(first, gain_part, 0.0)


def grads_kernel(
    got_ref, grad_ref, retained_ref, state_in_ref, state_grads_ref, col_ref, row_ref,
    queries_ref, keys_ref, values_ref,
):
    for c in range(CHUNKS):
        column, line, last = chunk_decay(col_ref, row_ref, c)
        q, k, v = part(got_ref, c, 0), part(got_ref, c, 1), part(got_ref, c, 2)
        grad = grad_ref[c]
        scores = nt(grad, v)
        grad_retained = (scores * (SCALE * chunk_weight(column, line))).astype(BF16)
        from_start = SCALE * jnp.exp(column)
        queries = nn(grad_retained, k) + from_start * nt(grad, state_in_ref[c])
        queries_ref[c] = queries.astype(BF16)
        keys = tn(grad_retained, q)
        values = tn(retained_ref[c], grad)
        if c < CHUNKS - 1:
            to_end = jnp.exp(last - column)
            keys = keys + to_end * nt(v, state_grads_ref[c])
            values = values + to_end * nn(k, state_grads_ref[c])
        keys_ref[c] = keys
        values_ref[c] = values


def last_kernel(
    half_ref, got_ref, queries_ref, keys_ref, values_ref, middle_ref, col_ref, row_ref, out_ref
):
    middle = jnp.where(half_ref[0] > 0, 0.0, middle_ref[...].astype(F32)).astype(BF16)
    after = jnp.zeros((1, 1), F32)
    for c in reversed(range(CHUNKS)):
        column, line, last = chunk_decay(col_ref, row_ref, c)
        to_end = jnp.exp(after + (last - column))
        after = after + last
        k, v = part(got_ref, c, 1), part(got_ref, c, 2)
        keys = keys_ref[c] + to_end * nt(v, middle)
        values = values_ref[c] + to_end * nn(k, middle)
        per = CHUNK // TOK
        for n, item in enumerate((queries_ref[c], keys.astype(BF16), values.astype(BF16))):
            out_ref[c * per : (c + 1) * per, n * TOK : (n + 1) * TOK, :] = item.reshape(per, TOK, 256)


def unpack_kernel(got_ref, queries_ref, keys_ref, values_ref):
    for h in range(HEADS):
        cols = slice(h * KD, (h + 1) * KD)
        for n, ref in enumerate((queries_ref, keys_ref, values_ref)):
            ref[:, cols] = got_ref[h, n * TOK : (n + 1) * TOK, :]


def sum_over_dp(value):
    size = lax.axis_size("dp")

    def fetch(item, step):
        return lax.ppermute(item, "dp", [(i, i ^ step) for i in range(size)])

    step = 1
    while step < size:
        if step * 4 <= size:
            one, two, three = fetch(value, step), fetch(value, 2 * step), fetch(value, 3 * step)
            value = (value + one) + (two + three)
            step *= 4
        else:
            value = value + fetch(value, step)
            step *= 2
    return value


def shards(queries, key_vectors, values, grad_out, log_decay, norm_gain):
    place = lax.axis_index("ctx")
    blocks = lax.axis_size("ctx")
    halves = [list(range(GROUP)), list(range(GROUP, 2 * GROUP))]
    swap = [(i, i ^ GROUP) for i in range(blocks)]
    half = (place // GROUP).astype(jnp.int32).reshape(1)
    gain = lax.dynamic_slice_in_dim(norm_gain.reshape(HEADS, VD), place % GROUP, 1, 0)
    square = (CHUNKS, CHUNK, 256)

    packed = call(pack_kernel, [((GROUP, ROWS, 256), BF16)])(
        queries[0], key_vectors[0], values[0], grad_out[0], log_decay[0]
    )[0]
    got = lax.all_to_all(packed, "ctx", 0, 0, axis_index_groups=halves, tiled=True)
    total, states, column, line = call(
        state_kernel,
        [((KD, VD), BF16), ((CHUNKS, KD, VD), F32), ((CHUNK, 8), F32), ((8, CHUNK), F32)],
        [pltpu.VMEM((8, CHUNK), F32)],
    )(got)
    middle = lax.ppermute(total, "ctx", swap)
    retained, output = call(local_kernel, [(square, BF16), (square, F32)])(
        got, states, column, line
    )
    grad, state_in, state_grads, total_grad, gain_part = call(
        output_kernel,
        [(square, BF16), (square, BF16), (square, BF16), ((KD, VD), BF16), ((8, VD), F32)],
        [pltpu.VMEM((CHUNKS, KD, VD), F32)],
        smem=(0,),
    )(half, got, states, output, middle, column, line, gain)
    middle_grad = lax.ppermute(total_grad, "ctx", swap)
    gains = lax.all_to_all(
        jnp.broadcast_to(gain_part[None], (blocks, 8, VD)), "ctx", 0, 0, tiled=True
    )
    gain_sum = sum_over_dp(gains[:GROUP, 0] + gains[GROUP:, 0])
    grad_queries, grad_keys, grad_values = call(
        grads_kernel, [(square, BF16), (square, F32), (square, F32)]
    )(got, grad, retained, state_in, state_grads, column, line)
    back = call(last_kernel, [((GROUP, BACK, 256), BF16)], smem=(0,))(
        half, got, grad_queries, grad_keys, grad_values, middle_grad, column, line
    )[0]
    back = lax.all_to_all(back, "ctx", 0, 0, axis_index_groups=halves, tiled=True)
    results = call(unpack_kernel, [((TOK, HEADS * KD), BF16)] * 3)(back)
    grad_gain = (gain_sum / lax.axis_size("dp")).reshape(HEADS * VD)
    return (*(item[None] for item in results), grad_gain)


def solution(mesh):
    return jax.shard_map(
        shards,
        mesh=mesh,
        in_specs=(
            P("dp", "ctx", None),
            P("dp", "ctx", None),
            P("dp", "ctx", None),
            P("dp", "ctx", None),
            P("dp", None, "ctx"),
            P(),
        ),
        out_specs=(P("dp", "ctx", None), P("dp", "ctx", None), P("dp", "ctx", None), P()),
        check_vma=False,
    )
```

time: 353 us -> 126 us (0.36)
  the two profiles are of different devices: /device:TPU:1 before, /device:TPU:6 now
where the time goes in v1:
time: 126 us; the launch traced here: 125 us
  starting transfers between devices  52.9 us (42%)
  blocking collectives  32.3 us (26%)
  waiting for transfers between devices  14.7 us (12%)
  local copies, waits for them, and re-layouts  13.9 us (11%)
  Pallas kernels  9.04 us (7%)
    ppermute x7, starting transfers between devices, fetch(): return lax.ppermute(item, 'dp', [(i, i ^ step) for i in range(size)])  34 us
    all_to_all x1, blocking collectives, shards(): lax.all_to_all(packed, 'ctx', 0, 0, axis_index_groups=halves, tiled=True)  32.3 us
    unnamed x32, local copies, waits for them, and re-layouts  13.2 us
    ppermute x7, waiting for transfers between devices, fetch(): return lax.ppermute(item, 'dp', [(i, i ^ step) for i in range(size)])  10.3 us
    pallas_call x7, Pallas kernels, run(): pl.pallas_call(kernel, out_shape=[jax.ShapeDtypeStruct(shape, kind) for s...  9.04 us
    all_to_all x1, starting transfers between devices, shards(): lax.all_to_all(jnp.broadcast_to(gain_part[None], (blocks, 8, VD)), 'ctx',...  6.79 us
    all_to_all x1, starting transfers between devices, shards(): lax.all_to_all(back, 'ctx', 0, 0, axis_index_groups=halves, tiled=True)  5.71 us
    ppermute x1, waiting for transfers between devices, shards(): middle = lax.ppermute(total, 'ctx', swap)  4.49 us
  transfers between devices with their start and end apart: 11, of which 4 were waited for; matrix products, arithmetic and copies ran while one was open for 2% of the time, Pallas kernels for 2%

profile of v1, /device:TPU:6, one launch (start us, length us, event | category | flops | bytes accessed | tf_op | source)
XLA Modules:
  0.0 124.7 jit_solution(10534640905389316078)
XLA Ops:
  0.6 0.0 copy-start.1
  0.6 1.0 copy-done.1
  1.7 1.0 copy-done.2
  2.7 1.0 copy-done.3
  3.8 1.0 copy-done.4
  4.8 0.7 copy-done.13
  5.5 0.2 shard_map.93
  5.7 32.3 %all_to_all.15.got_ref = bf16[8,528,256]{2,1,0:T(8,128)(2,1)S(1)} all-to-all(bf16[8,528,256]{2,1,0:T(8,128)(2,1)S(1)} %shard_map.93), channel_id=1, replica_groups={{0,1,2,3,4,5,6,7},{8,9,10,11,12,13,14,15},{16,17,18,19,20,21,22,23},{24..., dimensions={0} | all-to-all | bytes 4325376 | tf_op jit(solution)/shard_map/all_to_all | solution.py:245
  38.0 1.9 %shard_map.94 = (bf16[256,256]{1,0:T(8,128)(2,1)}, f32[4,256,256]{2,1,0:T(8,128)S(1)}, f32[256,8]{1,0:T(8,128)S(1)}, f32[8,256]{1,0:T(8,128)S(1)}) custom-call(bf16[8,528,256]{2,1,0:T(8,128)(2,1)S(1)} %all_to_all.15.got_ref), custom_call_target="tpu_custom_call" | custom-call | tf_op jit(solution)/shard_map/pallas_call | solution.py:45
  39.9 3.2 %collective-permute-start = (bf16[256,256]{1,0:T(8,128)(2,1)}, bf16[256,256]{1,0:T(8,128)(2,1)S(1)}, u32[]{:S(2)}, u32[]{:S(2)}) collective-permute-start(bf16[256,256]{1,0:T(8,128)(2,1)} %get-tuple-element.25), channel_id=1, source_target_pairs={{0,8},{1,9},{2,10},{3,11},{4,12},{5,13},{6,14},{7,15},{8,0},{9,1},... | collective-permute-start | bytes 393224 | tf_op jit(solution)/shard_map/ppermute | solution.py:251
  43.2 0.8 shard_map.95
  43.9 0.0 copy-start.5
  44.0 4.5 %collective-permute-done.middle_ref = bf16[256,256]{1,0:T(8,128)(2,1)S(1)} collective-permute-done((bf16[256,256]{1,0:T(8,128)(2,1)}, bf16[256,256]{1,0:T(8,128)(2,1)S(1)}, u32[]{:S(2)}, u32[]{:S(2)}) %collective-permute-start) | collective-permute-done | bytes 131104 | tf_op jit(solution)/shard_map/ppermute | solution.py:251
  48.4 2.6 %shard_map.96 = (bf16[4,256,256]{2,1,0:T(8,128)(2,1)S(1)}, bf16[4,256,256]{2,1,0:T(8,128)(2,1)S(1)}, bf16[4,256,256]{2,1,0:T(8,128)(2,1)S(1)}, bf16[256,256]{1,0:T(8,128)(2,1)}, f32[8,256]{1,0:T(8,128)S(1)}) custom-call(s32[1]{0:T(128)} %bitcast.half_ref, bf16[8,528,256]{2,1,0:T(8,128)(2,1)S(1)} %all_to_all.15.got_ref, ...), custom_call_target="tpu_custom_call" | custom-call | tf_op jit(solution)/shard_map/pallas_call | solution.py:45
  51.1 0.8 copy-done.7
  51.9 0.8 copy-done.9
  52.7 0.8 copy-done.11
  53.5 3.2 %collective-permute-start.1 = (bf16[256,256]{1,0:T(8,128)(2,1)}, bf16[256,256]{1,0:T(8,128)(2,1)S(1)}, u32[]{:S(2)}, u32[]{:S(2)}) collective-permute-start(bf16[256,256]{1,0:T(8,128)(2,1)} %get-tuple-element.33), channel_id=1, source_target_pairs={{0,8},{1,9},{2,10},{3,11},{4,12},{5,13},{6,14},{7,15},{8,0},{9,1},... | collective-permute-start | bytes 393224 | tf_op jit(solution)/shard_map/ppermute | solution.py:261
  56.7 0.7 broadcast_in_dim.18
  57.3 6.8 %all-to-all-start.2 = ((f32[16,8,256]{2,1,0:T(8,128)}), f32[16,8,256]{2,1,0:T(8,128)}, u32[]{:S(2)}, u32[]{:S(2)}) async-start(f32[16,8,256]{2,1,0:T(8,128)} %broadcast_in_dim.18), calls=%async_computation.2 | async-start | bytes 262144 | tf_op jit(solution)/shard_map/all_to_all | solution.py:262
  64.1 1.0 copy-done.6
  65.2 1.0 copy-done.8
  66.2 1.0 copy-done.10
  67.3 1.0 copy-done.12
  68.3 1.4 %shard_map.97 = (bf16[4,256,256]{2,1,0:T(8,128)(2,1)S(1)}, f32[4,256,256]{2,1,0:T(8,128)S(1)}, f32[4,256,256]{2,1,0:T(8,128)S(1)}) custom-call(bf16[8,528,256]{2,1,0:T(8,128)(2,1)S(1)} %all_to_all.15.got_ref, bf16[4,256,256]{2,1,0:T(8,128)(2,1)S(1)} %copy-done.8, bf16[4,256,256]{2,1,0:T(8,128)(2,1)S(1)} %copy-done.6, bf16[4,256,256]{2,1,0:T(8,128)(2,1)S(1)} %copy-done.10, ...), custom_call_target="tpu_custom_call" | custom-call | tf_op jit(solution)/shard_map/pallas_call | solution.py:45
  69.7 0.0 collective-permute-done.1.middle_ref
  69.8 0.9 shard_map.98
  70.6 1.2 copy-done
  71.8 0.0 all-to-all-done.2
  71.8 5.7 %all-to-all-start.1 = ((bf16[8,384,256]{2,1,0:T(8,128)(2,1)}), bf16[8,384,256]{2,1,0:T(8,128)(2,1)S(1)}, u32[]{:S(2)}, u32[]{:S(2)}) async-start(bf16[8,384,256]{2,1,0:T(8,128)(2,1)} %copy-done), calls=%async_computation.1 | async-start | bytes 3145728 | tf_op jit(solution)/shard_map/all_to_all | solution.py:272
  77.5 0.9 slice_add_fusion
  78.4 3.8 %collective-permute-start.3 = (f32[8,256]{1,0:T(8,128)S(1)}, f32[8,256]{1,0:T(8,128)S(1)}, u32[]{:S(2)}, u32[]{:S(2)}) collective-permute-start(f32[8,256]{1,0:T(8,128)S(1)} %bitcast.23), channel_id=1, source_target_pairs={{0,32},{16,48},{32,0},{48,16},{64,96},{80,112},{96,64},{112,80},{1... | collective-permute-start | bytes 24584 | tf_op jit(solution)/shard_map/ppermute | solution.py:219
  82.2 1.9 %collective-permute-start.4 = (f32[8,256]{1,0:T(8,128)S(1)}, f32[8,256]{1,0:T(8,128)S(1)}, u32[]{:S(2)}, u32[]{:S(2)}) collective-permute-start(f32[8,256]{1,0:T(8,128)S(1)} %bitcast.24), channel_id=1, source_target_pairs={{0,48},{16,32},{32,16},{48,0},{64,112},{80,96},{96,80},{112,64},{1... | collective-permute-start | bytes 24584 | tf_op jit(solution)/shard_map/ppermute | solution.py:219
  84.2 2.1 %collective-permute-start.2 = (f32[8,256]{1,0:T(8,128)S(1)}, f32[8,256]{1,0:T(8,128)S(1)}, u32[]{:S(2)}, u32[]{:S(2)}) collective-permute-start(f32[8,256]{1,0:T(8,128)S(1)} %bitcast.25), channel_id=1, source_target_pairs={{0,16},{16,0},{32,48},{48,32},{64,80},{80,64},{96,112},{112,96},{1... | collective-permute-start | bytes 24584 | tf_op jit(solution)/shard_map/ppermute | solution.py:219
  86.3 0.0 collective-permute-done.3
  86.3 0.9 collective-permute-done.4
  87.2 0.0 collective-permute-done.2
  87.2 11.8 %collective-permute-start.7 = (f32[8,256]{1,0:T(8,128)S(1)}, f32[8,256]{1,0:T(8,128)S(1)}, u32[]{:S(2)}, u32[]{:S(2)}) collective-permute-start(f32[8,256]{1,0:T(8,128)S(1)} %add_add_fusion.1), channel_id=1, source_target_pairs={{0,192},{16,208},{32,224},{48,240},{64,128},{80,144},{96,160},{112... | collective-permute-start | bytes 24584 | tf_op jit(solution)/shard_map/ppermute | solution.py:219
  99.0 1.9 %collective-permute-start.6 = (f32[8,256]{1,0:T(8,128)S(1)}, f32[8,256]{1,0:T(8,128)S(1)}, u32[]{:S(2)}, u32[]{:S(2)}) collective-permute-start(f32[8,256]{1,0:T(8,128)S(1)} %add_add_fusion.1), channel_id=1, source_target_pairs={{0,128},{16,144},{32,160},{48,176},{64,192},{80,208},{96,224},{112... | collective-permute-start | bytes 24584 | tf_op jit(solution)/shard_map/ppermute | solution.py:219
  101.0 2.5 %collective-permute-start.5 = (f32[8,256]{1,0:T(8,128)S(1)}, f32[8,256]{1,0:T(8,128)S(1)}, u32[]{:S(2)}, u32[]{:S(2)}) collective-permute-start(f32[8,256]{1,0:T(8,128)S(1)} %add_add_fusion.1), channel_id=1, source_target_pairs={{0,64},{16,80},{32,96},{48,112},{64,0},{80,16},{96,32},{112,48},{1... | collective-permute-start | bytes 24584 | tf_op jit(solution)/shard_map/ppermute | solution.py:219
  103.5 0.0 collective-permute-done.7
  103.5 5.0 %collective-permute-done.6 = f32[8,256]{1,0:T(8,128)S(1)} collective-permute-done((f32[8,256]{1,0:T(8,128)S(1)}, f32[8,256]{1,0:T(8,128)S(1)}, u32[]{:S(2)}, u32[]{:S(2)}) %collective-permute-start.6) | collective-permute-done | bytes 8224 | tf_op jit(solution)/shard_map/ppermute | solution.py:219
  108.5 0.0 collective-permute-done.5
  108.5 10.0 %collective-permute-start.8 = (f32[8,256]{1,0:T(8,128)S(1)}, f32[8,256]{1,0:T(8,128)S(1)}, u32[]{:S(2)}, u32[]{:S(2)}) collective-permute-start(f32[8,256]{1,0:T(8,128)S(1)} %add_add_fusion), channel_id=1, source_target_pairs={{0,256},{16,272},{32,288},{48,304},{64,320},{80,336},{96,352},{112... | collective-permute-start | bytes 24584 | tf_op jit(solution)/shard_map/ppermute | solution.py:219
  118.5 4.3 %collective-permute-done.8 = f32[8,256]{1,0:T(8,128)S(1)} collective-permute-done((f32[8,256]{1,0:T(8,128)S(1)}, f32[8,256]{1,0:T(8,128)S(1)}, u32[]{:S(2)}, u32[]{:S(2)}) %collective-permute-start.8) | collective-permute-done | bytes 8224 | tf_op jit(solution)/shard_map/ppermute | solution.py:219
  122.8 0.6 copy.11
  123.4 0.0 all-to-all-done.1.got_ref
  123.4 1.3 %shard_map.99 = (bf16[128,2048]{1,0:T(8,128)(2,1)}, bf16[128,2048]{1,0:T(8,128)(2,1)}, bf16[128,2048]{1,0:T(8,128)(2,1)}) custom-call(bf16[8,384,256]{2,1,0:T(8,128)(2,1)S(1)} %all-to-all-done.1.got_ref), custom_call_target="tpu_custom_call" | custom-call | tf_op jit(solution)/shard_map/pallas_call | solution.py:45
  (21 shorter events, 0.1 us)
Async XLA Ops:
  0.6 1.0 copy-start.1
  1.7 1.0 copy-start.2
  2.7 1.0 copy-start.3
  3.8 1.0 copy-start.4
  4.8 0.7 copy-start.13
  38.0 5.1 %copy-start.14 = (f32[2048]{0:T(1024)S(1)}, f32[2048]{0:T(1024)}, u32[]{:S(2)}) copy-start(f32[2048]{0:T(1024)} %param.11) | copy-start | bytes 24580
  39.9 8.6 %collective-permute-start = (bf16[256,256]{1,0:T(8,128)(2,1)}, bf16[256,256]{1,0:T(8,128)(2,1)S(1)}, u32[]{:S(2)}, u32[]{:S(2)}) collective-permute-start(bf16[256,256]{1,0:T(8,128)(2,1)} %get-tuple-element.25), channel_id=1, source_target_pairs={{0,8},{1,9},{2,10},{3,11},{4,12},{5,13},{6,14},{7,15},{8,0},{9,1},... | collective-permute-start | bytes 393224 | tf_op jit(solution)/shard_map/ppermute | solution.py:251
  43.9 7.1 %copy-start.5 = (bf16[4,256,256]{2,1,0:T(8,128)(2,1)}, bf16[4,256,256]{2,1,0:T(8,128)(2,1)S(1)}, u32[]{:S(2)}) copy-start(bf16[4,256,256]{2,1,0:T(8,128)(2,1)S(1)} %get-tuple-element.27.retained_ref) | copy-start | bytes 1572868
  51.1 0.8 copy-start.7
  51.9 0.8 copy-start.9
  52.7 0.8 copy-start.11
  53.5 16.3 %collective-permute-start.1 = (bf16[256,256]{1,0:T(8,128)(2,1)}, bf16[256,256]{1,0:T(8,128)(2,1)S(1)}, u32[]{:S(2)}, u32[]{:S(2)}) collective-permute-start(bf16[256,256]{1,0:T(8,128)(2,1)} %get-tuple-element.33), channel_id=1, source_target_pairs={{0,8},{1,9},{2,10},{3,11},{4,12},{5,13},{6,14},{7,15},{8,0},{9,1},... | collective-permute-start | bytes 393224 | tf_op jit(solution)/shard_map/ppermute | solution.py:261
  57.3 14.5 %all-to-all-start.2 = ((f32[16,8,256]{2,1,0:T(8,128)}), f32[16,8,256]{2,1,0:T(8,128)}, u32[]{:S(2)}, u32[]{:S(2)}) async-start(f32[16,8,256]{2,1,0:T(8,128)} %broadcast_in_dim.18), calls=%async_computation.2 | async-start | bytes 262144 | tf_op jit(solution)/shard_map/all_to_all | solution.py:262
  64.1 1.0 copy-start.6
  65.2 1.0 copy-start.8
  66.2 1.0 copy-start.10
  67.3 1.0 copy-start.12
  70.6 1.2 copy-start
  71.8 51.6 %all-to-all-start.1 = ((bf16[8,384,256]{2,1,0:T(8,128)(2,1)}), bf16[8,384,256]{2,1,0:T(8,128)(2,1)S(1)}, u32[]{:S(2)}, u32[]{:S(2)}) async-start(bf16[8,384,256]{2,1,0:T(8,128)(2,1)} %copy-done), calls=%async_computation.1 | async-start | bytes 3145728 | tf_op jit(solution)/shard_map/all_to_all | solution.py:272
  78.4 7.9 %collective-permute-start.3 = (f32[8,256]{1,0:T(8,128)S(1)}, f32[8,256]{1,0:T(8,128)S(1)}, u32[]{:S(2)}, u32[]{:S(2)}) collective-permute-start(f32[8,256]{1,0:T(8,128)S(1)} %bitcast.23), channel_id=1, source_target_pairs={{0,32},{16,48},{32,0},{48,16},{64,96},{80,112},{96,64},{112,80},{1... | collective-permute-start | bytes 24584 | tf_op jit(solution)/shard_map/ppermute | solution.py:219
  82.2 5.0 %collective-permute-start.4 = (f32[8,256]{1,0:T(8,128)S(1)}, f32[8,256]{1,0:T(8,128)S(1)}, u32[]{:S(2)}, u32[]{:S(2)}) collective-permute-start(f32[8,256]{1,0:T(8,128)S(1)} %bitcast.24), channel_id=1, source_target_pairs={{0,48},{16,32},{32,16},{48,0},{64,112},{80,96},{96,80},{112,64},{1... | collective-permute-start | bytes 24584 | tf_op jit(solution)/shard_map/ppermute | solution.py:219
  84.2 3.1 %collective-permute-start.2 = (f32[8,256]{1,0:T(8,128)S(1)}, f32[8,256]{1,0:T(8,128)S(1)}, u32[]{:S(2)}, u32[]{:S(2)}) collective-permute-start(f32[8,256]{1,0:T(8,128)S(1)} %bitcast.25), channel_id=1, source_target_pairs={{0,16},{16,0},{32,48},{48,32},{64,80},{80,64},{96,112},{112,96},{1... | collective-permute-start | bytes 24584 | tf_op jit(solution)/shard_map/ppermute | solution.py:219
  87.2 16.2 %collective-permute-start.7 = (f32[8,256]{1,0:T(8,128)S(1)}, f32[8,256]{1,0:T(8,128)S(1)}, u32[]{:S(2)}, u32[]{:S(2)}) collective-permute-start(f32[8,256]{1,0:T(8,128)S(1)} %add_add_fusion.1), channel_id=1, source_target_pairs={{0,192},{16,208},{32,224},{48,240},{64,128},{80,144},{96,160},{112... | collective-permute-start | bytes 24584 | tf_op jit(solution)/shard_map/ppermute | solution.py:219
  99.0 9.5 %collective-permute-start.6 = (f32[8,256]{1,0:T(8,128)S(1)}, f32[8,256]{1,0:T(8,128)S(1)}, u32[]{:S(2)}, u32[]{:S(2)}) collective-permute-start(f32[8,256]{1,0:T(8,128)S(1)} %add_add_fusion.1), channel_id=1, source_target_pairs={{0,128},{16,144},{32,160},{48,176},{64,192},{80,208},{96,224},{112... | collective-permute-start | bytes 24584 | tf_op jit(solution)/shard_map/ppermute | solution.py:219
  101.0 7.5 %collective-permute-start.5 = (f32[8,256]{1,0:T(8,128)S(1)}, f32[8,256]{1,0:T(8,128)S(1)}, u32[]{:S(2)}, u32[]{:S(2)}) collective-permute-start(f32[8,256]{1,0:T(8,128)S(1)} %add_add_fusion.1), channel_id=1, source_target_pairs={{0,64},{16,80},{32,96},{48,112},{64,0},{80,16},{96,32},{112,48},{1... | collective-permute-start | bytes 24584 | tf_op jit(solution)/shard_map/ppermute | solution.py:219
  108.5 14.3 %collective-permute-start.8 = (f32[8,256]{1,0:T(8,128)S(1)}, f32[8,256]{1,0:T(8,128)S(1)}, u32[]{:S(2)}, u32[]{:S(2)}) collective-permute-start(f32[8,256]{1,0:T(8,128)S(1)} %add_add_fusion), channel_id=1, source_target_pairs={{0,256},{16,272},{32,288},{48,304},{64,320},{80,336},{96,352},{112... | collective-permute-start | bytes 24584 | tf_op jit(solution)/shard_map/ppermute | solution.py:219

commit v2 on v1

v2 whole, which is shorter than its diff:
```python
import jax
import jax.numpy as jnp
from jax import lax
from jax.experimental import pallas as pl
from jax.experimental.pallas import tpu as pltpu
from jax.sharding import PartitionSpec as P

HEADS = 8
KD = 256
VD = 256
EPSILON = 1e-05

TOK = 128
GROUP = 8
CHUNK = 256
CHUNKS = GROUP * TOK // CHUNK
ROWS = 4 * TOK + 16
BACK = 3 * TOK

F32 = jnp.float32
BF16 = jnp.bfloat16
SCALE = KD ** (-0.5)


def nn(a, b):
    return lax.dot_general(a, b, (((1,), (0,)), ((), ())), preferred_element_type=F32)


def nt(a, b):
    return lax.dot_general(a, b, (((1,), (1,)), ((), ())), preferred_element_type=F32)


def tn(a, b):
    return lax.dot_general(a, b, (((0,), (0,)), ((), ())), preferred_element_type=F32)


def call(kernel, outs, scratch=(), places=None, out_place=None, grant=16):
    def run(*args):
        where = places or {}
        return pl.pallas_call(
            kernel,
            out_shape=[jax.ShapeDtypeStruct(shape, kind) for shape, kind in outs],
            in_specs=[
                pl.BlockSpec(memory_space=where.get(i, pltpu.VMEM)) for i in range(len(args))
            ],
            out_specs=[pl.BlockSpec(memory_space=out_place or pltpu.VMEM) for _ in outs],
            scratch_shapes=list(scratch),
            compiler_params=pltpu.CompilerParams(vmem_limit_bytes=grant * 1024 * 1024),
        )(*args)

    return run


def pack_kernel(q_ref, k_ref, v_ref, g_ref, decay_ref, out_ref, decay_buf, sems, decay_sem):
    fetch = pltpu.make_async_copy(decay_ref, decay_buf, decay_sem)
    fetch.start()
    copies = []
    for n, ref in enumerate((q_ref, k_ref, v_ref, g_ref)):
        for h in range(HEADS):
            copies.append(
                pltpu.make_async_copy(
                    ref.at[:, h * KD : (h + 1) * KD],
                    out_ref.at[h, n * TOK : (n + 1) * TOK, :],
                    sems.at[n * HEADS + h],
                )
            )
    for copy in copies:
        copy.start()
    fetch.wait()
    row = lax.broadcasted_iota(jnp.int32, (16, 256), 0)
    for h in range(HEADS):
        decay = decay_buf[h : h + 1, :]
        high = decay.astype(BF16).astype(F32)
        rest = decay - high
        middle = rest.astype(BF16).astype(F32)
        low = rest - middle
        first = jnp.concatenate([high, middle], axis=1)
        second = jnp.concatenate([low, jnp.zeros_like(low)], axis=1)
        pieces = jnp.where(row == 0, first, jnp.where(row == 1, second, 0.0))
        out_ref[h, 4 * TOK :, :] = pieces.astype(BF16)
    for copy in copies:
        copy.wait()


def part(ref, c, n):
    per = CHUNK // TOK
    return ref[c * per : (c + 1) * per, n * TOK : (n + 1) * TOK, :].reshape(CHUNK, 256)


def chunk_decay(col_ref, row_ref, c):
    column = col_ref[:, c : c + 1]
    line = row_ref[c : c + 1, :]
    return column, line, line[:, CHUNK - 1 :]


def chunk_weight(column, line):
    t = lax.broadcasted_iota(jnp.int32, (CHUNK, CHUNK), 0)
    s = lax.broadcasted_iota(jnp.int32, (CHUNK, CHUNK), 1)
    return jnp.where(t >= s, jnp.exp(jnp.minimum(column - line, 0.0)), 0.0)


def state_kernel(got_ref, total_ref, states_ref, col_ref, row_ref, decay_ref):
    decay_ref[...] = jnp.zeros_like(decay_ref)
    for i in range(GROUP):
        pieces = got_ref[i, 4 * TOK :, :].astype(F32)
        decay = pieces[0:1, :TOK] + pieces[0:1, TOK:] + pieces[1:2, :TOK]
        c, j = divmod(i * TOK, CHUNK)
        decay_ref[c : c + 1, j : j + TOK] = decay
    decay = decay_ref[...]
    t = lax.broadcasted_iota(jnp.int32, (CHUNK, CHUNK), 0)
    s = lax.broadcasted_iota(jnp.int32, (CHUNK, CHUNK), 1)
    lower = (t >= s).astype(F32)
    exact = dict(precision=lax.Precision.HIGHEST, preferred_element_type=F32)
    row_ref[...] = lax.dot_general(decay, lower, (((1,), (1,)), ((), ())), **exact)
    col_ref[...] = lax.dot_general(lower, decay, (((1,), (1,)), ((), ())), **exact)
    carried = jnp.zeros((KD, VD), F32)
    for c in range(CHUNKS):
        states_ref[c] = carried
        column, line, last = chunk_decay(col_ref, row_ref, c)
        key_tail = (part(got_ref, c, 1).astype(F32) * jnp.exp(last - column)).astype(BF16)
        carried = jnp.exp(last) * carried + tn(key_tail, part(got_ref, c, 2))
    total_ref[...] = carried.astype(BF16)


def local_kernel(got_ref, states_ref, col_ref, row_ref, retained_ref, output_ref):
    for c in range(CHUNKS):
        column, line, last = chunk_decay(col_ref, row_ref, c)
        q = part(got_ref, c, 0)
        scores = nt(q, part(got_ref, c, 1))
        retained = (scores * (SCALE * chunk_weight(column, line))).astype(BF16)
        retained_ref[c] = retained
        output = nn(retained, part(got_ref, c, 2))
        if c:
            tail = (q.astype(F32) * (SCALE * jnp.exp(column))).astype(BF16)
            output = output + nn(tail, states_ref[c].astype(BF16))
        output_ref[c] = output


def output_kernel(
    where_ref, got_ref, states_ref, retained_ref, output_ref, middle_ref, col_ref, row_ref, gain_ref,
    queries_ref, keys_ref, values_ref, total_ref, gain_part_ref, block_grads,
):
    gain = gain_ref[0:1, :]
    middle = jnp.where(where_ref[0] > 0, middle_ref[...].astype(F32), 0.0)
    middle_low = middle.astype(BF16)
    before = jnp.zeros((1, 1), F32)
    gain_part = jnp.zeros((1, VD), F32)
    for c in range(CHUNKS):
        column, line, last = chunk_decay(col_ref, row_ref, c)
        q, k, v = part(got_ref, c, 0), part(got_ref, c, 1), part(got_ref, c, 2)
        from_start = SCALE * jnp.exp(column)
        tail = (q.astype(F32) * from_start).astype(BF16)
        state_in = (states_ref[c] + jnp.exp(before) * middle).astype(BF16)
        output = output_ref[c] + jnp.exp(before) * nn(tail, middle_low)
        before = before + last
        centred = output - jnp.mean(output, axis=1, keepdims=True)
        inverse = lax.rsqrt(jnp.mean(centred * centred, axis=1, keepdims=True) + EPSILON)
        normed = centred * inverse
        wide = part(got_ref, c, 3).astype(F32)
        gain_part = gain_part + jnp.sum(wide * normed, axis=0, keepdims=True)
        scaled = wide * gain
        grad = inverse * (
            scaled
            - jnp.mean(scaled, axis=1, keepdims=True)
            - normed * jnp.mean(scaled * normed, axis=1, keepdims=True)
        )
        grad = grad.astype(BF16)
        block_grads[c] = tn(tail, grad)
        scores = nt(grad, v)
        grad_retained = (scores * (SCALE * chunk_weight(column, line))).astype(BF16)
        queries = nn(grad_retained, k) + from_start * nt(grad, state_in)
        queries_ref[c] = queries.astype(BF16)
        keys_ref[c] = tn(grad_retained, q)
        values_ref[c] = tn(retained_ref[c], grad)
    carried = jnp.zeros((KD, VD), F32)
    for c in reversed(range(CHUNKS)):
        column, _, last = chunk_decay(col_ref, row_ref, c)
        if c < CHUNKS - 1:
            to_end = jnp.exp(last - column)
            after = carried.astype(BF16)
            keys_ref[c] += to_end * nt(part(got_ref, c, 2), after)
            values_ref[c] += to_end * nn(part(got_ref, c, 1), after)
        carried = jnp.exp(last) * carried + block_grads[c]
    total_ref[...] = carried.astype(BF16)
    mine = lax.broadcasted_iota(jnp.int32, (HEADS, VD), 0) == where_ref[1]
    gain_part_ref[...] = jnp.where(mine, gain_part, 0.0)


def last_kernel(
    where_ref, got_ref, queries_ref, keys_ref, values_ref, middle_ref, col_ref, row_ref,
    out_ref, out_buf, sems,
):
    middle = jnp.where(where_ref[0] > 0, 0.0, middle_ref[...].astype(F32)).astype(BF16)
    after = jnp.zeros((1, 1), F32)
    per = CHUNK // TOK
    copies = []
    for c in reversed(range(CHUNKS)):
        column, line, last = chunk_decay(col_ref, row_ref, c)
        to_end = jnp.exp(after + (last - column))
        after = after + last
        k, v = part(got_ref, c, 1), part(got_ref, c, 2)
        keys = keys_ref[c] + to_end * nt(v, middle)
        values = values_ref[c] + to_end * nn(k, middle)
        blocks = slice(c * per, (c + 1) * per)
        for n, item in enumerate((queries_ref[c], keys.astype(BF16), values.astype(BF16))):
            out_buf[blocks, n * TOK : (n + 1) * TOK, :] = item.reshape(per, TOK, 256)
        copies.append(pltpu.make_async_copy(out_buf.at[blocks], out_ref.at[blocks], sems.at[c]))
        copies[-1].start()
    for copy in copies:
        copy.wait()


def unpack_kernel(got_ref, queries_ref, keys_ref, values_ref, sems):
    copies = []
    for n, ref in enumerate((queries_ref, keys_ref, values_ref)):
        for h in range(HEADS):
            copies.append(
                pltpu.make_async_copy(
                    got_ref.at[h, n * TOK : (n + 1) * TOK, :],
                    ref.at[:, h * KD : (h + 1) * KD],
                    sems.at[n * HEADS + h],
                )
            )
    for copy in copies:
        copy.start()
    for copy in copies:
        copy.wait()


def shards(queries, key_vectors, values, grad_out, log_decay, norm_gain):
    place = lax.axis_index("ctx")
    blocks = lax.axis_size("ctx")
    halves = [list(range(GROUP)), list(range(GROUP, 2 * GROUP))]
    swap = [(i, i ^ GROUP) for i in range(blocks)]
    where = jnp.stack([place // GROUP, place % GROUP]).astype(jnp.int32)
    gain = lax.dynamic_slice_in_dim(norm_gain.reshape(HEADS, VD), place % GROUP, 1, 0)
    square = (CHUNKS, CHUNK, 256)

    packed = call(
        pack_kernel,
        [((GROUP, ROWS, 256), BF16)],
        [
            pltpu.VMEM((HEADS, TOK), F32),
            pltpu.SemaphoreType.DMA((4 * HEADS,)),
            pltpu.SemaphoreType.DMA,
        ],
        places={i: pltpu.HBM for i in range(5)},
        grant=56,
    )(queries[0], key_vectors[0], values[0], grad_out[0], log_decay[0])[0]
    got = lax.all_to_all(packed, "ctx", 0, 0, axis_index_groups=halves, tiled=True)
    total, states, column, line = call(
        state_kernel,
        [((KD, VD), BF16), ((CHUNKS, KD, VD), F32), ((CHUNK, 8), F32), ((8, CHUNK), F32)],
        [pltpu.VMEM((8, CHUNK), F32)],
    )(got)
    middle = lax.ppermute(total, "ctx", swap)
    retained, output = call(local_kernel, [(square, BF16), (square, F32)])(
        got, states, column, line
    )
    grad_queries, grad_keys, grad_values, total_grad, gain_part = call(
        output_kernel,
        [(square, BF16), (square, F32), (square, F32), ((KD, VD), BF16), ((HEADS, VD), F32)],
        [pltpu.VMEM((CHUNKS, KD, VD), F32)],
        places={0: pltpu.SMEM},
    )(where, got, states, retained, output, middle, column, line, gain)
    middle_grad = lax.ppermute(total_grad, "ctx", swap)
    gains = lax.all_to_all(
        jnp.broadcast_to(gain_part[None], (blocks, HEADS, VD)), "ctx", 0, 0, tiled=True
    )
    back = call(
        last_kernel,
        [((GROUP, BACK, 256), BF16)],
        [pltpu.VMEM((GROUP, BACK, 256), BF16), pltpu.SemaphoreType.DMA((CHUNKS,))],
        places={0: pltpu.SMEM},
        out_place=pltpu.HBM,
    )(where, got, grad_queries, grad_keys, grad_values, middle_grad, column, line)[0]
    back = lax.all_to_all(back, "ctx", 0, 0, axis_index_groups=halves, tiled=True)
    gain_all = lax.all_gather(jnp.sum(gains, axis=0), "dp")
    results = call(
        unpack_kernel,
        [((TOK, HEADS * KD), BF16)] * 3,
        [pltpu.SemaphoreType.DMA((3 * HEADS,))],
        places={0: pl.ANY},
        out_place=pltpu.HBM,
    )(back)
    grad_gain = (jnp.sum(gain_all, axis=0) / lax.axis_size("dp")).reshape(HEADS * VD)
    return (*(item[None] for item in results), grad_gain)


def solution(mesh):
    return jax.shard_map(
        shards,
        mesh=mesh,
        in_specs=(
            P("dp", "ctx", None),
            P("dp", "ctx", None),
            P("dp", "ctx", None),
            P("dp", "ctx", None),
            P("dp", None, "ctx"),
            P(),
        ),
        out_specs=(P("dp", "ctx", None), P("dp", "ctx", None), P("dp", "ctx", None), P()),
        check_vma=False,
    )
```

time: 126 us -> 117 us (0.929)
  the two profiles are of different devices: /device:TPU:6 before, /device:TPU:1 now
where the time goes in v2:
time: 117 us; the launch traced here: 116 us
  blocking collectives  39.6 us (34%)
  waiting for transfers between devices  27.5 us (24%)
  starting transfers between devices  25.4 us (22%)
  Pallas kernels  14.4 us (12%)
  local copies, waits for them, and re-layouts  8.7 us (7%)
    all_gather x1, blocking collectives, shards(): gain_all = lax.all_gather(jnp.sum(gains, axis=0), 'dp')  39.6 us
    all_to_all x1, waiting for transfers between devices, shards(): lax.all_to_all(packed, 'ctx', 0, 0, axis_index_groups=halves, tiled=True)  25.8 us
    pallas_call x6, Pallas kernels, run(): pl.pallas_call(kernel, out_shape=[jax.ShapeDtypeStruct(shape, kind) for s...  14.4 us
    unnamed x17, local copies, waits for them, and re-layouts  8.02 us
    all_to_all x1, starting transfers between devices, shards(): lax.all_to_all(packed, 'ctx', 0, 0, axis_index_groups=halves, tiled=True)  5.96 us
    ppermute x1, starting transfers between devices, shards(): middle = lax.ppermute(total, 'ctx', swap)  5.36 us
    ppermute x1, starting transfers between devices, shards(): middle_grad = lax.ppermute(total_grad, 'ctx', swap)  5.22 us
    all_to_all x1, starting transfers between devices, shards(): lax.all_to_all(back, 'ctx', 0, 0, axis_index_groups=halves, tiled=True)  5.04 us
  transfers between devices with their start and end apart: 5, of which 2 were waited for; matrix products, arithmetic and copies ran while one was open for 1% of the time, Pallas kernels for 3%

profile of v2, /device:TPU:1, one launch (start us, length us, event | category | flops | bytes accessed | tf_op | source)
XLA Modules:
  0.0 116.4 jit_solution(2787576461655280836)
XLA Ops:
  0.6 3.2 %shard_map.93 = bf16[8,528,256]{2,1,0:T(8,128)(2,1)} custom-call(bf16[128,2048]{1,0:T(8,128)(2,1)} %bitcast.15, bf16[128,2048]{1,0:T(8,128)(2,1)} %bitcast.16, bf16[128,2048]{1,0:T(8,128)(2,1)} %bitcast.17, bf16[128,2048]{1,0:T(8,128)(2,1)} %bitcast.18, f32[8,128]{1,0:T(8,128)} %bitcast.20), custom_call_target="tpu_custom_call" | custom-call | tf_op jit(solution)/shard_map/pallas_call | solution.py:40
  3.9 6.0 %all-to-all-start = ((bf16[8,528,256]{2,1,0:T(8,128)(2,1)}), bf16[8,528,256]{2,1,0:T(8,128)(2,1)S(1)}, u32[]{:S(2)}, u32[]{:S(2)}) async-start(bf16[8,528,256]{2,1,0:T(8,128)(2,1)} %shard_map.93), calls=%async_computation | async-start | bytes 4325376 | tf_op jit(solution)/shard_map/all_to_all | solution.py:250
  9.8 0.0 copy-start.7
  9.9 25.8 %all-to-all-done.got_ref = bf16[8,528,256]{2,1,0:T(8,128)(2,1)S(1)} async-done(((bf16[8,528,256]{2,1,0:T(8,128)(2,1)}), bf16[8,528,256]{2,1,0:T(8,128)(2,1)S(1)}, u32[]{:S(2)}, u32[]{:S(2)}) %all-to-all-start) | async-done | bytes 2162720 | tf_op jit(solution)/shard_map/all_to_all | solution.py:250
  35.7 1.9 %shard_map.94 = (bf16[256,256]{1,0:T(8,128)(2,1)}, f32[4,256,256]{2,1,0:T(8,128)S(1)}, f32[256,8]{1,0:T(8,128)S(1)}, f32[8,256]{1,0:T(8,128)S(1)}) custom-call(bf16[8,528,256]{2,1,0:T(8,128)(2,1)S(1)} %all-to-all-done.got_ref), custom_call_target="tpu_custom_call" | custom-call | tf_op jit(solution)/shard_map/pallas_call | solution.py:40
  37.6 5.4 %collective-permute-start = (bf16[256,256]{1,0:T(8,128)(2,1)}, bf16[256,256]{1,0:T(8,128)(2,1)S(1)}, u32[]{:S(2)}, u32[]{:S(2)}) collective-permute-start(bf16[256,256]{1,0:T(8,128)(2,1)} %get-tuple-element.23), channel_id=1, source_target_pairs={{0,8},{1,9},{2,10},{3,11},{4,12},{5,13},{6,14},{7,15},{8,0},{9,1},... | collective-permute-start | bytes 393224 | tf_op jit(solution)/shard_map/ppermute | solution.py:256
  42.9 0.1 pad_add_fusion.where_ref
  43.0 0.0 copy-done.7
  43.0 0.8 shard_map.95
  43.8 1.7 %collective-permute-done.middle_ref = bf16[256,256]{1,0:T(8,128)(2,1)S(1)} collective-permute-done((bf16[256,256]{1,0:T(8,128)(2,1)}, bf16[256,256]{1,0:T(8,128)(2,1)S(1)}, u32[]{:S(2)}, u32[]{:S(2)}) %collective-permute-start) | collective-permute-done | bytes 131104 | tf_op jit(solution)/shard_map/ppermute | solution.py:256
  45.5 4.7 %shard_map.96 = (bf16[4,256,256]{2,1,0:T(8,128)(2,1)S(1)}, f32[4,256,256]{2,1,0:T(8,128)S(1)}, f32[4,256,256]{2,1,0:T(8,128)S(1)}, bf16[256,256]{1,0:T(8,128)(2,1)}, f32[8,256]{1,0:T(8,128)S(1)}) custom-call(s32[2]{0:T(128)S(1)} %pad_add_fusion.where_ref, bf16[8,528,256]{2,1,0:T(8,128)(2,1)S(1)} %all-to-all-done.got_ref, ...), custom_call_target="tpu_custom_call" | custom-call | tf_op jit(solution)/shard_map/pallas_call | solution.py:40
  50.2 0.0 copy-start.1
  50.2 1.0 copy-done.1
  51.2 0.0 copy-start.3
  51.2 1.0 copy-done.3
  52.2 0.0 copy-start.5
  52.2 0.8 copy-done.5
  53.0 5.2 %collective-permute-start.1 = (bf16[256,256]{1,0:T(8,128)(2,1)}, bf16[256,256]{1,0:T(8,128)(2,1)S(1)}, u32[]{:S(2)}, u32[]{:S(2)}) collective-permute-start(bf16[256,256]{1,0:T(8,128)(2,1)} %get-tuple-element.27), channel_id=1, source_target_pairs={{0,8},{1,9},{2,10},{3,11},{4,12},{5,13},{6,14},{7,15},{8,0},{9,1},... | collective-permute-start | bytes 393224 | tf_op jit(solution)/shard_map/ppermute | solution.py:266
  58.2 0.7 broadcast_in_dim.18
  58.9 3.8 %all-to-all-start.2 = ((f32[16,8,256]{2,1,0:T(8,128)}), f32[16,8,256]{2,1,0:T(8,128)S(1)}, u32[]{:S(2)}, u32[]{:S(2)}) async-start(f32[16,8,256]{2,1,0:T(8,128)} %broadcast_in_dim.18), calls=%async_computation.2 | async-start | bytes 262144 | tf_op jit(solution)/shard_map/all_to_all | solution.py:267
  62.7 0.0 collective-permute-done.1.middle_ref
  62.7 0.0 copy-start.2
  62.7 1.2 %copy-done.2 = f32[4,256,256]{2,1,0:T(8,128)S(1)} copy-done((f32[4,256,256]{2,1,0:T(8,128)S(1)}, f32[4,256,256]{2,1,0:T(8,128)}, u32[]{:S(2)}) %copy-start.2) | copy-done | bytes 1048600
  63.9 0.0 copy-start.4
  63.9 1.2 %copy-done.4 = f32[4,256,256]{2,1,0:T(8,128)S(1)} copy-done((f32[4,256,256]{2,1,0:T(8,128)S(1)}, f32[4,256,256]{2,1,0:T(8,128)}, u32[]{:S(2)}) %copy-start.4) | copy-done | bytes 1048600
  65.2 0.0 copy-start.6
  65.2 1.0 copy-done.6
  66.2 2.4 %shard_map.97 = bf16[8,384,256]{2,1,0:T(8,128)(2,1)S(1)} custom-call(s32[2]{0:T(128)S(1)} %pad_add_fusion.where_ref, bf16[8,528,256]{2,1,0:T(8,128)(2,1)S(1)} %all-to-all-done.got_ref, bf16[4,256,256]{2,1,0:T(8,128)(2,1)S(1)} %copy-done.6, f32[4,256,256]{2,1,0:T(8,128)S(1)} %copy-done.2, f32[4,256,256]{2,1,0:T(8,128)S(1)} %copy-done.4, ...), custom_call_target="tpu_custom_call" | custom-call | tf_op jit(solution)/shard_map/pallas_call | solution.py:40
  68.6 0.0 copy-start
  68.6 1.2 copy-done
  69.8 0.0 all-to-all-done.2
  69.8 5.0 %all-to-all-start.1 = ((bf16[8,384,256]{2,1,0:T(8,128)(2,1)}), bf16[8,384,256]{2,1,0:T(8,128)(2,1)S(1)}, u32[]{:S(2)}, u32[]{:S(2)}) async-start(bf16[8,384,256]{2,1,0:T(8,128)(2,1)} %copy-done), calls=%async_computation.1 | async-start | bytes 3145728 | tf_op jit(solution)/shard_map/all_to_all | solution.py:277
  74.8 39.6 %all-gather = f32[256,256]{1,0:T(8,128)S(1)} all-gather(f32[8,256]{1,0:T(8,128)S(1)} %reduce_sum.18), channel_id=2, replica_groups=mesh['dp'=32,'ctx'=16] {'dp'}, dimensions={0}, use_global_device_ids=true | all-gather | bytes 270336 | tf_op jit(solution)/shard_map/all_gather | solution.py:278
  114.5 0.6 copy.10
  115.1 0.0 all-to-all-done.1.got_ref
  115.1 1.3 %shard_map.98 = (bf16[128,2048]{1,0:T(8,128)(2,1)}, bf16[128,2048]{1,0:T(8,128)(2,1)}, bf16[128,2048]{1,0:T(8,128)(2,1)}) custom-call(bf16[8,384,256]{2,1,0:T(8,128)(2,1)S(1)} %all-to-all-done.1.got_ref), custom_call_target="tpu_custom_call" | custom-call | tf_op jit(solution)/shard_map/pallas_call | solution.py:40
  (5 shorter events, 0.1 us)
Async XLA Ops:
  3.9 31.8 %all-to-all-start = ((bf16[8,528,256]{2,1,0:T(8,128)(2,1)}), bf16[8,528,256]{2,1,0:T(8,128)(2,1)S(1)}, u32[]{:S(2)}, u32[]{:S(2)}) async-start(bf16[8,528,256]{2,1,0:T(8,128)(2,1)} %shard_map.93), calls=%async_computation | async-start | bytes 4325376 | tf_op jit(solution)/shard_map/all_to_all | solution.py:250
  9.8 33.2 %copy-start.7 = (f32[2048]{0:T(1024)S(1)}, f32[2048]{0:T(1024)}, u32[]{:S(2)}) copy-start(f32[2048]{0:T(1024)} %param.11) | copy-start | bytes 24580
  37.6 7.9 %collective-permute-start = (bf16[256,256]{1,0:T(8,128)(2,1)}, bf16[256,256]{1,0:T(8,128)(2,1)S(1)}, u32[]{:S(2)}, u32[]{:S(2)}) collective-permute-start(bf16[256,256]{1,0:T(8,128)(2,1)} %get-tuple-element.23), channel_id=1, source_target_pairs={{0,8},{1,9},{2,10},{3,11},{4,12},{5,13},{6,14},{7,15},{8,0},{9,1},... | collective-permute-start | bytes 393224 | tf_op jit(solution)/shard_map/ppermute | solution.py:256
  50.2 1.0 copy-start.1
  51.2 1.0 copy-start.3
  52.2 0.8 copy-start.5
  53.0 9.7 %collective-permute-start.1 = (bf16[256,256]{1,0:T(8,128)(2,1)}, bf16[256,256]{1,0:T(8,128)(2,1)S(1)}, u32[]{:S(2)}, u32[]{:S(2)}) collective-permute-start(bf16[256,256]{1,0:T(8,128)(2,1)} %get-tuple-element.27), channel_id=1, source_target_pairs={{0,8},{1,9},{2,10},{3,11},{4,12},{5,13},{6,14},{7,15},{8,0},{9,1},... | collective-permute-start | bytes 393224 | tf_op jit(solution)/shard_map/ppermute | solution.py:266
  58.9 10.9 %all-to-all-start.2 = ((f32[16,8,256]{2,1,0:T(8,128)}), f32[16,8,256]{2,1,0:T(8,128)S(1)}, u32[]{:S(2)}, u32[]{:S(2)}) async-start(f32[16,8,256]{2,1,0:T(8,128)} %broadcast_in_dim.18), calls=%async_computation.2 | async-start | bytes 262144 | tf_op jit(solution)/shard_map/all_to_all | solution.py:267
  62.7 1.2 %copy-start.2 = (f32[4,256,256]{2,1,0:T(8,128)S(1)}, f32[4,256,256]{2,1,0:T(8,128)}, u32[]{:S(2)}) copy-start(f32[4,256,256]{2,1,0:T(8,128)} %copy-done.1) | copy-start | bytes 3145732
  63.9 1.2 %copy-start.4 = (f32[4,256,256]{2,1,0:T(8,128)S(1)}, f32[4,256,256]{2,1,0:T(8,128)}, u32[]{:S(2)}) copy-start(f32[4,256,256]{2,1,0:T(8,128)} %copy-done.3) | copy-start | bytes 3145732
  65.2 1.0 copy-start.6
  68.6 1.2 %copy-start = (bf16[8,384,256]{2,1,0:T(8,128)(2,1)}, bf16[8,384,256]{2,1,0:T(8,128)(2,1)S(1)}, u32[]{:S(2)}) copy-start(bf16[8,384,256]{2,1,0:T(8,128)(2,1)S(1)} %shard_map.97) | copy-start | bytes 4718596
  69.8 45.3 %all-to-all-start.1 = ((bf16[8,384,256]{2,1,0:T(8,128)(2,1)}), bf16[8,384,256]{2,1,0:T(8,128)(2,1)S(1)}, u32[]{:S(2)}, u32[]{:S(2)}) async-start(bf16[8,384,256]{2,1,0:T(8,128)(2,1)} %copy-done), calls=%async_computation.1 | async-start | bytes 3145728 | tf_op jit(solution)/shard_map/all_to_all | solution.py:277

commit v3 on v2

--- a/solution.py
+++ b/solution.py
@@ -34,16 +34,26 @@
     return lax.dot_general(a, b, (((0,), (0,)), ((), ())), preferred_element_type=F32)
 
 
-def call(kernel, outs, scratch=(), places=None, out_place=None, grant=16):
+def call(kernel, outs, scratch=(), places=None, far=(), grant=16):
     def run(*args):
         where = places or {}
+        args = [
+            pltpu.with_memory_space_constraint(item, pltpu.HBM) if where.get(i) == pltpu.HBM else item
+            for i, item in enumerate(args)
+        ]
         return pl.pallas_call(
             kernel,
-            out_shape=[jax.ShapeDtypeStruct(shape, kind) for shape, kind in outs],
+            out_shape=[
+                (pltpu.HBM if i in far else jax.ShapeDtypeStruct)(shape, kind)
+                for i, (shape, kind) in enumerate(outs)
+            ],
             in_specs=[
                 pl.BlockSpec(memory_space=where.get(i, pltpu.VMEM)) for i in range(len(args))
             ],
-            out_specs=[pl.BlockSpec(memory_space=out_place or pltpu.VMEM) for _ in outs],
+            out_specs=[
+                pl.BlockSpec(memory_space=pltpu.HBM if i in far else pltpu.VMEM)
+                for i in range(len(outs))
+            ],
             scratch_shapes=list(scratch),
             compiler_params=pltpu.CompilerParams(vmem_limit_bytes=grant * 1024 * 1024),
         )(*args)
@@ -51,7 +61,9 @@
     return run
 
 
-def pack_kernel(q_ref, k_ref, v_ref, g_ref, decay_ref, out_ref, decay_buf, sems, decay_sem):
+def pack_kernel(
+    q_ref, k_ref, v_ref, g_ref, decay_ref, out_ref, decay_buf, pieces_buf, sems, decay_sem, pieces_sem
+):
     fetch = pltpu.make_async_copy(decay_ref, decay_buf, decay_sem)
     fetch.start()
     copies = []
@@ -77,14 +89,34 @@
         first = jnp.concatenate([high, middle], axis=1)
         second = jnp.concatenate([low, jnp.zeros_like(low)], axis=1)
         pieces = jnp.where(row == 0, first, jnp.where(row == 1, second, 0.0))
-        out_ref[h, 4 * TOK :, :] = pieces.astype(BF16)
+        pieces_buf[h] = pieces.astype(BF16)
+    store = pltpu.make_async_copy(pieces_buf, out_ref.at[:, 4 * TOK :, :], pieces_sem)
+    store.start()
     for copy in copies:
         copy.wait()
+    store.wait()
 
 
 def part(ref, c, n):
     per = CHUNK // TOK
     return ref[c * per : (c + 1) * per, n * TOK : (n + 1) * TOK, :].reshape(CHUNK, 256)
+
+
+def put(ref, c, n, item):
+    per = CHUNK // TOK
+    item = item.astype(BF16).reshape(per, TOK, 256)
+    ref[c * per : (c + 1) * per, n * TOK : (n + 1) * TOK, :] = item
+
+
+def rows_of(ref, c, n):
+    per = CHUNK // TOK
+    return ref.at[c * per : (c + 1) * per, n * TOK : (n + 1) * TOK, :]
+
+
+def send(source, target, sems, c, n):
+    copy = pltpu.make_async_copy(rows_of(source, c, n), rows_of(target, c, n), sems.at[n, c])
+    copy.start()
+    return copy
 
 
 def chunk_decay(col_ref, row_ref, c):
@@ -138,8 +170,9 @@
 
 def output_kernel(
     where_ref, got_ref, states_ref, retained_ref, output_ref, middle_ref, col_ref, row_ref, gain_ref,
-    queries_ref, keys_ref, values_ref, total_ref, gain_part_ref, block_grads,
+    out_ref, total_ref, gain_part_ref, back_ref, total_buf, block_grads, keys_acc, values_acc, sems,
 ):
+    copies = []
     gain = gain_ref[0:1, :]
     middle = jnp.where(where_ref[0] > 0, middle_ref[...].astype(F32), 0.0)
     middle_low = middle.astype(BF16)
@@ -169,43 +202,53 @@
         scores = nt(grad, v)
         grad_retained = (scores * (SCALE * chunk_weight(column, line))).astype(BF16)
         queries = nn(grad_retained, k) + from_start * nt(grad, state_in)
-        queries_ref[c] = queries.astype(BF16)
-        keys_ref[c] = tn(grad_retained, q)
-        values_ref[c] = tn(retained_ref[c], grad)
+        put(back_ref, c, 0, queries)
+        copies.append(send(back_ref, out_ref, sems, c, 0))
+        keys_acc[c] = tn(grad_retained, q)
+        values_acc[c] = tn(retained_ref[c], grad)
     carried = jnp.zeros((KD, VD), F32)
     for c in reversed(range(CHUNKS)):
         column, _, last = chunk_decay(col_ref, row_ref, c)
+        keys, values = keys_acc[c], values_acc[c]
         if c < CHUNKS - 1:
             to_end = jnp.exp(last - column)
             after = carried.astype(BF16)
-            keys_ref[c] += to_end * nt(part(got_ref, c, 2), after)
-            values_ref[c] += to_end * nn(part(got_ref, c, 1), after)
+            keys = keys + to_end * nt(part(got_ref, c, 2), after)
+            values = values + to_end * nn(part(got_ref, c, 1), after)
+        put(back_ref, c, 1, keys)
+        put(back_ref, c, 2, values)
+        copies.append(send(back_ref, out_ref, sems, c, 1))
+        copies.append(send(back_ref, out_ref, sems, c, 2))
         carried = jnp.exp(last) * carried + block_grads[c]
-    total_ref[...] = carried.astype(BF16)
+    total_buf[...] = carried.astype(BF16)
+    copies.append(pltpu.make_async_copy(total_buf, total_ref, sems.at[3, 0]))
+    copies[-1].start()
     mine = lax.broadcasted_iota(jnp.int32, (HEADS, VD), 0) == where_ref[1]
     gain_part_ref[...] = jnp.where(mine, gain_part, 0.0)
-
-
-def last_kernel(
-    where_ref, got_ref, queries_ref, keys_ref, values_ref, middle_ref, col_ref, row_ref,
-    out_ref, out_buf, sems,
-):
+    for copy in copies:
+        copy.wait()
+
+
+def last_kernel(where_ref, got_ref, back_ref, middle_ref, col_ref, row_ref, out_ref, buf, sems, out_sems):
+    fetches = {}
+    for c in reversed(range(CHUNKS)):
+        for n in range(3):
+            fetches[c, n] = send(back_ref, buf, sems, c, n)
     middle = jnp.where(where_ref[0] > 0, 0.0, middle_ref[...].astype(F32)).astype(BF16)
     after = jnp.zeros((1, 1), F32)
-    per = CHUNK // TOK
     copies = []
     for c in reversed(range(CHUNKS)):
         column, line, last = chunk_decay(col_ref, row_ref, c)
         to_end = jnp.exp(after + (last - column))
         after = after + last
         k, v = part(got_ref, c, 1), part(got_ref, c, 2)
-        keys = keys_ref[c] + to_end * nt(v, middle)
-        values = values_ref[c] + to_end * nn(k, middle)
-        blocks = slice(c * per, (c + 1) * per)
-        for n, item in enumerate((queries_ref[c], keys.astype(BF16), values.astype(BF16))):
-            out_buf[blocks, n * TOK : (n + 1) * TOK, :] = item.reshape(per, TOK, 256)
-        copies.append(pltpu.make_async_copy(out_buf.at[blocks], out_ref.at[blocks], sems.at[c]))
-        copies[-1].start()
+        keys, values = to_end * nt(v, middle), to_end * nn(k, middle)
+        for n in range(3):
+            fetches[c, n].wait()
+        put(buf, c, 1, part(buf, c, 1).astype(F32) + keys)
+        put(buf, c, 2, part(buf, c, 2).astype(F32) + values)
+        for n in range(3):
+            copies.append(send(buf, out_ref, out_sems, c, n))
     for copy in copies:
         copy.wait()
 
@@ -231,6 +274,9 @@
     place = lax.axis_index("ctx")
     blocks = lax.axis_size("ctx")
     halves = [list(range(GROUP)), list(range(GROUP, 2 * GROUP))]
+    size = lax.axis_size("dp")
+    planes = [list(range(2 * i * blocks, 2 * (i + 1) * blocks)) for i in range(size // 2)]
+    columns = [list(range(core, size, 2)) for core in range(2)]
     swap = [(i, i ^ GROUP) for i in range(blocks)]
     where = jnp.stack([place // GROUP, place % GROUP]).astype(jnp.int32)
     gain = lax.dynamic_slice_in_dim(norm_gain.reshape(HEADS, VD), place % GROUP, 1, 0)
@@ -241,11 +287,13 @@
         [((GROUP, ROWS, 256), BF16)],
         [
             pltpu.VMEM((HEADS, TOK), F32),
+            pltpu.VMEM((HEADS, 16, 256), BF16),
             pltpu.SemaphoreType.DMA((4 * HEADS,)),
+            pltpu.SemaphoreType.DMA,
             pltpu.SemaphoreType.DMA,
         ],
         places={i: pltpu.HBM for i in range(5)},
-        grant=56,
+        far=(0,),
     )(queries[0], key_vectors[0], values[0], grad_out[0], log_decay[0])[0]
     got = lax.all_to_all(packed, "ctx", 0, 0, axis_index_groups=halves, tiled=True)
     total, states, column, line = call(
@@ -257,33 +305,40 @@
     retained, output = call(local_kernel, [(square, BF16), (square, F32)])(
         got, states, column, line
     )
-    grad_queries, grad_keys, grad_values, total_grad, gain_part = call(
+    back, total_grad, gain_part = call(
         output_kernel,
-        [(square, BF16), (square, F32), (square, F32), ((KD, VD), BF16), ((HEADS, VD), F32)],
-        [pltpu.VMEM((CHUNKS, KD, VD), F32)],
+        [((GROUP, BACK, 256), BF16), ((KD, VD), BF16), ((HEADS, VD), F32)],
+        [
+            pltpu.VMEM((GROUP, BACK, 256), BF16),
+            pltpu.VMEM((KD, VD), BF16),
+            *[pltpu.VMEM((CHUNKS, 256, 256), F32)] * 3,
+            pltpu.SemaphoreType.DMA((4, CHUNKS)),
+        ],
         places={0: pltpu.SMEM},
+        far=(0, 1),
     )(where, got, states, retained, output, middle, column, line, gain)
     middle_grad = lax.ppermute(total_grad, "ctx", swap)
     gains = lax.all_to_all(
-        jnp.broadcast_to(gain_part[None], (blocks, HEADS, VD)), "ctx", 0, 0, tiled=True
+        jnp.broadcast_to(gain_part[None], (2 * blocks, HEADS, VD)),
+        ("dp", "ctx"), 0, 0, axis_index_groups=planes, tiled=True,
     )
     back = call(
         last_kernel,
         [((GROUP, BACK, 256), BF16)],
-        [pltpu.VMEM((GROUP, BACK, 256), BF16), pltpu.SemaphoreType.DMA((CHUNKS,))],
-        places={0: pltpu.SMEM},
-        out_place=pltpu.HBM,
-    )(where, got, grad_queries, grad_keys, grad_values, middle_grad, column, line)[0]
+        [pltpu.VMEM((GROUP, BACK, 256), BF16), *[pltpu.SemaphoreType.DMA((3, CHUNKS))] * 2],
+        places={0: pltpu.SMEM, 2: pltpu.HBM},
+        far=(0,),
+    )(where, got, back, middle_grad, column, line)[0]
     back = lax.all_to_all(back, "ctx", 0, 0, axis_index_groups=halves, tiled=True)
-    gain_all = lax.all_gather(jnp.sum(gains, axis=0), "dp")
+    gain_all = lax.all_gather(jnp.sum(gains, axis=0), "dp", axis_index_groups=columns)
     results = call(
         unpack_kernel,
         [((TOK, HEADS * KD), BF16)] * 3,
         [pltpu.SemaphoreType.DMA((3 * HEADS,))],
         places={0: pl.ANY},
-        out_place=pltpu.HBM,
+        far=(0, 1, 2),
     )(back)
-    grad_gain = (jnp.sum(gain_all, axis=0) / lax.axis_size("dp")).reshape(HEADS * VD)
+    grad_gain = (jnp.sum(gain_all, axis=0) / size).reshape(HEADS * VD)
     return (*(item[None] for item in results), grad_gain)
 
 

time: 117 us -> 177 us (1.51)
  the two profiles are of different devices: /device:TPU:1 before, /device:TPU:2 now
where the time goes in v3:
time: 177 us
  Pallas kernels  77.5 us (44%)
  blocking collectives  36.1 us (20%)
  waiting for transfers between devices  31.5 us (18%)
  starting transfers between devices  29.2 us (16%)
    pallas_call x6, Pallas kernels, run(): pl.pallas_call(kernel, out_shape=[(pltpu.HBM if i in far else jax.ShapeDt...  77.5 us
    all_gather x1, blocking collectives, shards(): lax.all_gather(jnp.sum(gains, axis=0), 'dp', axis_index_groups=columns)  36.1 us
    all_to_all x1, waiting for transfers between devices, shards(): lax.all_to_all(packed, 'ctx', 0, 0, axis_index_groups=halves, tiled=True)  22.7 us
    all_to_all x1, starting transfers between devices, shards(): lax.all_to_all(packed, 'ctx', 0, 0, axis_index_groups=halves, tiled=True)  9.45 us
    all_to_all x1, starting transfers between devices, shards(): lax.all_to_all(jnp.broadcast_to(gain_part[None], (2 * blocks, HEADS, VD))...  6.06 us
    all_to_all x1, starting transfers between devices, shards(): lax.all_to_all(back, 'ctx', 0, 0, axis_index_groups=halves, tiled=True)  5.72 us
    ppermute x1, waiting for transfers between devices, shards(): middle_grad = lax.ppermute(total_grad, 'ctx', swap)  5.17 us
    ppermute x1, starting transfers between devices, shards(): middle = lax.ppermute(total, 'ctx', swap)  4.02 us
  transfers between devices with their start and end apart: 5, of which 3 were waited for; matrix products, arithmetic and copies ran while one was open for 0% of the time, Pallas kernels for 2%

profile of v3, /device:TPU:2, one launch (start us, length us, event | category | flops | bytes accessed | tf_op | source)
XLA Modules:
  0.0 176.5 jit_solution(9021613445837861251)
XLA Ops:
  0.6 64.9 %shard_map.93 = bf16[8,528,256]{2,1,0:T(8,128)(2,1)} custom-call(bf16[128,2048]{1,0:T(8,128)(2,1)} %bitcast.15, bf16[128,2048]{1,0:T(8,128)(2,1)} %bitcast.16, bf16[128,2048]{1,0:T(8,128)(2,1)} %bitcast.17, bf16[128,2048]{1,0:T(8,128)(2,1)} %bitcast.18, f32[8,128]{1,0:T(8,128)} %bitcast.20), custom_call_target="tpu_custom_call" | custom-call | tf_op jit(solution)/shard_map/pallas_call | solution.py:44
  65.6 9.4 %all-to-all-start = ((bf16[8,528,256]{2,1,0:T(8,128)(2,1)}), bf16[8,528,256]{2,1,0:T(8,128)(2,1)S(1)}, u32[]{:S(2)}, u32[]{:S(2)}) async-start(bf16[8,528,256]{2,1,0:T(8,128)(2,1)} %shard_map.93), calls=%async_computation | async-start | bytes 4325376 | tf_op jit(solution)/shard_map/all_to_all | solution.py:298
  75.0 0.0 copy-start
  75.0 22.7 %all-to-all-done.got_ref = bf16[8,528,256]{2,1,0:T(8,128)(2,1)S(1)} async-done(((bf16[8,528,256]{2,1,0:T(8,128)(2,1)}), bf16[8,528,256]{2,1,0:T(8,128)(2,1)S(1)}, u32[]{:S(2)}, u32[]{:S(2)}) %all-to-all-start) | async-done | bytes 2162720 | tf_op jit(solution)/shard_map/all_to_all | solution.py:298
  97.7 1.9 %shard_map.94 = (bf16[256,256]{1,0:T(8,128)(2,1)}, f32[4,256,256]{2,1,0:T(8,128)S(1)}, f32[256,8]{1,0:T(8,128)S(1)}, f32[8,256]{1,0:T(8,128)S(1)}) custom-call(bf16[8,528,256]{2,1,0:T(8,128)(2,1)S(1)} %all-to-all-done.got_ref), custom_call_target="tpu_custom_call" | custom-call | tf_op jit(solution)/shard_map/pallas_call | solution.py:44
  99.6 4.0 %collective-permute-start = (bf16[256,256]{1,0:T(8,128)(2,1)}, bf16[256,256]{1,0:T(8,128)(2,1)S(1)}, u32[]{:S(2)}, u32[]{:S(2)}) collective-permute-start(bf16[256,256]{1,0:T(8,128)(2,1)} %get-tuple-element.21), channel_id=1, source_target_pairs={{0,8},{1,9},{2,10},{3,11},{4,12},{5,13},{6,14},{7,15},{8,0},{9,1},... | collective-permute-start | bytes 393224 | tf_op jit(solution)/shard_map/ppermute | solution.py:304
  103.6 0.1 pad_add_fusion.where_ref
  103.7 0.0 copy-done
  103.7 0.8 shard_map.95
  104.5 3.6 %collective-permute-done.middle_ref = bf16[256,256]{1,0:T(8,128)(2,1)S(1)} collective-permute-done((bf16[256,256]{1,0:T(8,128)(2,1)}, bf16[256,256]{1,0:T(8,128)(2,1)S(1)}, u32[]{:S(2)}, u32[]{:S(2)}) %collective-permute-start) | collective-permute-done | bytes 131104 | tf_op jit(solution)/shard_map/ppermute | solution.py:304
  108.1 5.0 %shard_map.96 = (bf16[8,384,256]{2,1,0:T(8,128)(2,1)}, bf16[256,256]{1,0:T(8,128)(2,1)}, f32[8,256]{1,0:T(8,128)S(1)}) custom-call(s32[2]{0:T(128)S(1)} %pad_add_fusion.where_ref, bf16[8,528,256]{2,1,0:T(8,128)(2,1)S(1)} %all-to-all-done.got_ref, f32[4,256,256]{2,1,0:T(8,128)S(1)} %get-tuple-element.16.states_ref, ...), custom_call_target="tpu_custom_call" | custom-call | tf_op jit(solution)/shard_map/pallas_call | solution.py:44
  113.1 0.7 broadcast_in_dim.18
  113.9 6.1 %all-to-all-start.2 = ((f32[32,8,256]{2,1,0:T(8,128)}), f32[32,8,256]{2,1,0:T(8,128)S(1)}, u32[]{:S(2)}, u32[]{:S(2)}) async-start(f32[32,8,256]{2,1,0:T(8,128)} %broadcast_in_dim.18), calls=%async_computation.2 | async-start | bytes 524288 | tf_op jit(solution)/shard_map/all_to_all | solution.py:321
  119.9 4.0 %collective-permute-start.1 = (bf16[256,256]{1,0:T(8,128)(2,1)}, bf16[256,256]{1,0:T(8,128)(2,1)S(1)}, u32[]{:S(2)}, u32[]{:S(2)}) collective-permute-start(bf16[256,256]{1,0:T(8,128)(2,1)} %get-tuple-element.23), channel_id=1, source_target_pairs={{0,8},{1,9},{2,10},{3,11},{4,12},{5,13},{6,14},{7,15},{8,0},{9,1},... | collective-permute-start | bytes 393224 | tf_op jit(solution)/shard_map/ppermute | solution.py:320
  123.9 5.2 %collective-permute-done.1.middle_ref = bf16[256,256]{1,0:T(8,128)(2,1)S(1)} collective-permute-done((bf16[256,256]{1,0:T(8,128)(2,1)}, bf16[256,256]{1,0:T(8,128)(2,1)S(1)}, u32[]{:S(2)}, u32[]{:S(2)}) %collective-permute-start.1) | collective-permute-done | bytes 131104 | tf_op jit(solution)/shard_map/ppermute | solution.py:320
  129.1 3.6 %shard_map.97 = bf16[8,384,256]{2,1,0:T(8,128)(2,1)} custom-call(s32[2]{0:T(128)S(1)} %pad_add_fusion.where_ref, bf16[8,528,256]{2,1,0:T(8,128)(2,1)S(1)} %all-to-all-done.got_ref, bf16[8,384,256]{2,1,0:T(8,128)(2,1)} %get-tuple-element.22.back_ref, bf16[256,256]{1,0:T(8,128)(2,1)S(1)} %collective-permute-done.1.middle_ref, ...), custom_call_target="tpu_custom_call" | custom-call | tf_op jit(solution)/shard_map/pallas_call | solution.py:44
  132.7 0.0 all-to-all-done.2
  132.7 5.7 %all-to-all-start.1 = ((bf16[8,384,256]{2,1,0:T(8,128)(2,1)}), bf16[8,384,256]{2,1,0:T(8,128)(2,1)S(1)}, u32[]{:S(2)}, u32[]{:S(2)}) async-start(bf16[8,384,256]{2,1,0:T(8,128)(2,1)} %shard_map.97), calls=%async_computation.1 | async-start | bytes 3145728 | tf_op jit(solution)/shard_map/all_to_all | solution.py:332
  138.4 36.1 %all-gather = f32[128,256]{1,0:T(8,128)S(1)} all-gather(f32[8,256]{1,0:T(8,128)S(1)} %reduce_sum.18), channel_id=2, replica_groups={{0,32,64,96,128,160,192,224,256,288,320,352,384,416,448,480},{16,48,80,..., dimensions={0}, use_global_device_ids=true | all-gather | bytes 139264 | tf_op jit(solution)/shard_map/all_gather | solution.py:333
  174.6 0.6 copy.10
  175.2 0.0 all-to-all-done.1.got_ref
  175.2 1.3 shard_map.98
  (5 shorter events, 0.1 us)
Async XLA Ops:
  65.6 32.1 %all-to-all-start = ((bf16[8,528,256]{2,1,0:T(8,128)(2,1)}), bf16[8,528,256]{2,1,0:T(8,128)(2,1)S(1)}, u32[]{:S(2)}, u32[]{:S(2)}) async-start(bf16[8,528,256]{2,1,0:T(8,128)(2,1)} %shard_map.93), calls=%async_computation | async-start | bytes 4325376 | tf_op jit(solution)/shard_map/all_to_all | solution.py:298
  75.0 28.7 %copy-start = (f32[2048]{0:T(1024)S(1)}, f32[2048]{0:T(1024)}, u32[]{:S(2)}) copy-start(f32[2048]{0:T(1024)} %param.11) | copy-start | bytes 24580
  99.6 8.6 %collective-permute-start = (bf16[256,256]{1,0:T(8,128)(2,1)}, bf16[256,256]{1,0:T(8,128)(2,1)S(1)}, u32[]{:S(2)}, u32[]{:S(2)}) collective-permute-start(bf16[256,256]{1,0:T(8,128)(2,1)} %get-tuple-element.21), channel_id=1, source_target_pairs={{0,8},{1,9},{2,10},{3,11},{4,12},{5,13},{6,14},{7,15},{8,0},{9,1},... | collective-permute-start | bytes 393224 | tf_op jit(solution)/shard_map/ppermute | solution.py:304
  113.9 18.8 %all-to-all-start.2 = ((f32[32,8,256]{2,1,0:T(8,128)}), f32[32,8,256]{2,1,0:T(8,128)S(1)}, u32[]{:S(2)}, u32[]{:S(2)}) async-start(f32[32,8,256]{2,1,0:T(8,128)} %broadcast_in_dim.18), calls=%async_computation.2 | async-start | bytes 524288 | tf_op jit(solution)/shard_map/all_to_all | solution.py:321
  119.9 9.2 %collective-permute-start.1 = (bf16[256,256]{1,0:T(8,128)(2,1)}, bf16[256,256]{1,0:T(8,128)(2,1)S(1)}, u32[]{:S(2)}, u32[]{:S(2)}) collective-permute-start(bf16[256,256]{1,0:T(8,128)(2,1)} %get-tuple-element.23), channel_id=1, source_target_pairs={{0,8},{1,9},{2,10},{3,11},{4,12},{5,13},{6,14},{7,15},{8,0},{9,1},... | collective-permute-start | bytes 393224 | tf_op jit(solution)/shard_map/ppermute | solution.py:320
  132.7 42.5 %all-to-all-start.1 = ((bf16[8,384,256]{2,1,0:T(8,128)(2,1)}), bf16[8,384,256]{2,1,0:T(8,128)(2,1)S(1)}, u32[]{:S(2)}, u32[]{:S(2)}) async-start(bf16[8,384,256]{2,1,0:T(8,128)(2,1)} %shard_map.97), calls=%async_computation.1 | async-start | bytes 3145728 | tf_op jit(solution)/shard_map/all_to_all | solution.py:332

commit v4 on v3

--- a/solution.py
+++ b/solution.py
@@ -34,7 +34,7 @@
     return lax.dot_general(a, b, (((0,), (0,)), ((), ())), preferred_element_type=F32)
 
 
-def call(kernel, outs, scratch=(), places=None, far=(), grant=16):
+def call(kernel, outs, scratch=(), places=None, far=(), cost=None, aliases=None):
     def run(*args):
         where = places or {}
         args = [
@@ -55,28 +55,31 @@
                 for i in range(len(outs))
             ],
             scratch_shapes=list(scratch),
-            compiler_params=pltpu.CompilerParams(vmem_limit_bytes=grant * 1024 * 1024),
+            compiler_params=pltpu.CompilerParams(vmem_limit_bytes=16 * 1024 * 1024),
+            cost_estimate=cost and pl.CostEstimate(flops=cost[0], bytes_accessed=cost[1], transcendentals=0),
+            input_output_aliases=aliases or {},
         )(*args)
 
     return run
 
 
 def pack_kernel(
-    q_ref, k_ref, v_ref, g_ref, decay_ref, out_ref, decay_buf, pieces_buf, sems, decay_sem, pieces_sem
+    q_ref, k_ref, v_ref, g_ref, decay_ref, out_ref, buf, decay_buf, sems, decay_sem, out_sems
 ):
     fetch = pltpu.make_async_copy(decay_ref, decay_buf, decay_sem)
     fetch.start()
-    copies = []
-    for n, ref in enumerate((q_ref, k_ref, v_ref, g_ref)):
-        for h in range(HEADS):
-            copies.append(
-                pltpu.make_async_copy(
-                    ref.at[:, h * KD : (h + 1) * KD],
-                    out_ref.at[h, n * TOK : (n + 1) * TOK, :],
-                    sems.at[n * HEADS + h],
-                )
+    copies = [
+        [
+            pltpu.make_async_copy(
+                ref.at[:, h * KD : (h + 1) * KD],
+                buf.at[h, n * TOK : (n + 1) * TOK, :],
+                sems.at[h, n],
             )
-    for copy in copies:
+            for n, ref in enumerate((q_ref, k_ref, v_ref, g_ref))
+        ]
+        for h in range(HEADS)
+    ]
+    for copy in sum(copies, []):
         copy.start()
     fetch.wait()
     row = lax.broadcasted_iota(jnp.int32, (16, 256), 0)
@@ -89,12 +92,15 @@
         first = jnp.concatenate([high, middle], axis=1)
         second = jnp.concatenate([low, jnp.zeros_like(low)], axis=1)
         pieces = jnp.where(row == 0, first, jnp.where(row == 1, second, 0.0))
-        pieces_buf[h] = pieces.astype(BF16)
-    store = pltpu.make_async_copy(pieces_buf, out_ref.at[:, 4 * TOK :, :], pieces_sem)
-    store.start()
-    for copy in copies:
-        copy.wait()
-    store.wait()
+        buf[h, 4 * TOK :, :] = pieces.astype(BF16)
+    stores = []
+    for h in range(HEADS):
+        for copy in copies[h]:
+            copy.wait()
+        stores.append(pltpu.make_async_copy(buf.at[h], out_ref.at[h], out_sems.at[h]))
+        stores[-1].start()
+    for store in stores:
+        store.wait()
 
 
 def part(ref, c, n):
@@ -229,10 +235,15 @@
         copy.wait()
 
 
+def spread_kernel(gain_ref, out_ref):
+    for i in range(out_ref.shape[0]):
+        out_ref[i] = gain_ref[...]
+
+
 def last_kernel(where_ref, got_ref, back_ref, middle_ref, col_ref, row_ref, out_ref, buf, sems, out_sems):
     fetches = {}
     for c in reversed(range(CHUNKS)):
-        for n in range(3):
+        for n in (1, 2):
             fetches[c, n] = send(back_ref, buf, sems, c, n)
     middle = jnp.where(where_ref[0] > 0, 0.0, middle_ref[...].astype(F32)).astype(BF16)
     after = jnp.zeros((1, 1), F32)
@@ -241,13 +252,11 @@
         column, line, last = chunk_decay(col_ref, row_ref, c)
         to_end = jnp.exp(after + (last - column))
         after = after + last
-        k, v = part(got_ref, c, 1), part(got_ref, c, 2)
-        keys, values = to_end * nt(v, middle), to_end * nn(k, middle)
-        for n in range(3):
+        keys = to_end * nt(part(got_ref, c, 2), middle)
+        values = to_end * nn(part(got_ref, c, 1), middle)
+        for n, item in ((1, keys), (2, values)):
             fetches[c, n].wait()
-        put(buf, c, 1, part(buf, c, 1).astype(F32) + keys)
-        put(buf, c, 2, part(buf, c, 2).astype(F32) + values)
-        for n in range(3):
+            put(buf, c, n, part(buf, c, n).astype(F32) + item)
             copies.append(send(buf, out_ref, out_sems, c, n))
     for copy in copies:
         copy.wait()
@@ -275,8 +284,6 @@
     blocks = lax.axis_size("ctx")
     halves = [list(range(GROUP)), list(range(GROUP, 2 * GROUP))]
     size = lax.axis_size("dp")
-    planes = [list(range(2 * i * blocks, 2 * (i + 1) * blocks)) for i in range(size // 2)]
-    columns = [list(range(core, size, 2)) for core in range(2)]
     swap = [(i, i ^ GROUP) for i in range(blocks)]
     where = jnp.stack([place // GROUP, place % GROUP]).astype(jnp.int32)
     gain = lax.dynamic_slice_in_dim(norm_gain.reshape(HEADS, VD), place % GROUP, 1, 0)
@@ -286,11 +293,11 @@
         pack_kernel,
         [((GROUP, ROWS, 256), BF16)],
         [
+            pltpu.VMEM((GROUP, ROWS, 256), BF16),
             pltpu.VMEM((HEADS, TOK), F32),
-            pltpu.VMEM((HEADS, 16, 256), BF16),
-            pltpu.SemaphoreType.DMA((4 * HEADS,)),
+            pltpu.SemaphoreType.DMA((HEADS, 4)),
             pltpu.SemaphoreType.DMA,
-            pltpu.SemaphoreType.DMA,
+            pltpu.SemaphoreType.DMA((HEADS,)),
         ],
         places={i: pltpu.HBM for i in range(5)},
         far=(0,),
@@ -319,8 +326,8 @@
     )(where, got, states, retained, output, middle, column, line, gain)
     middle_grad = lax.ppermute(total_grad, "ctx", swap)
     gains = lax.all_to_all(
-        jnp.broadcast_to(gain_part[None], (2 * blocks, HEADS, VD)),
-        ("dp", "ctx"), 0, 0, axis_index_groups=planes, tiled=True,
+        call(spread_kernel, [((blocks, HEADS, VD), F32)], cost=(4 * 10**9, 2**20))(gain_part)[0],
+        "ctx", 0, 0, tiled=True,
     )
     back = call(
         last_kernel,
@@ -328,9 +335,10 @@
         [pltpu.VMEM((GROUP, BACK, 256), BF16), *[pltpu.SemaphoreType.DMA((3, CHUNKS))] * 2],
         places={0: pltpu.SMEM, 2: pltpu.HBM},
         far=(0,),
+        aliases={2: 0},
     )(where, got, back, middle_grad, column, line)[0]
     back = lax.all_to_all(back, "ctx", 0, 0, axis_index_groups=halves, tiled=True)
-    gain_all = lax.all_gather(jnp.sum(gains, axis=0), "dp", axis_index_groups=columns)
+    gain_all = lax.all_gather(jnp.sum(gains, axis=0), "dp")
     results = call(
         unpack_kernel,
         [((TOK, HEADS * KD), BF16)] * 3,

time: 177 us -> 113 us (0.64)
  the two profiles are of different devices: /device:TPU:2 before, /device:TPU:1 now
where the time goes in v4:
time: 113 us
  blocking collectives  40.2 us (36%)
  waiting for transfers between devices  30.9 us (27%)
  starting transfers between devices  23.9 us (21%)
  Pallas kernels  16.1 us (14%)
    all_gather x1, blocking collectives, shards(): gain_all = lax.all_gather(jnp.sum(gains, axis=0), 'dp')  40.2 us
    all_to_all x1, waiting for transfers between devices, shards(): lax.all_to_all(packed, 'ctx', 0, 0, axis_index_groups=halves, tiled=True)  25.8 us
    pallas_call x7, Pallas kernels, run(): pl.pallas_call(kernel, out_shape=[(pltpu.HBM if i in far else jax.ShapeDt...  16.1 us
    all_to_all x1, starting transfers between devices, shards(): lax.all_to_all(packed, 'ctx', 0, 0, axis_index_groups=halves, tiled=True)  5.96 us
    ppermute x1, starting transfers between devices, shards(): middle = lax.ppermute(total, 'ctx', swap)  5.36 us
    ppermute x1, starting transfers between devices, shards(): middle_grad = lax.ppermute(total_grad, 'ctx', swap)  5.21 us
    all_to_all x1, starting transfers between devices, shards(): lax.all_to_all(call(spread_kernel, [((blocks, HEADS, VD), F32)], cost=(4...  3.79 us
    all_to_all x1, starting transfers between devices, shards(): lax.all_to_all(back, 'ctx', 0, 0, axis_index_groups=halves, tiled=True)  3.58 us
  transfers between devices with their start and end apart: 5, of which 3 were waited for; matrix products, arithmetic and copies ran while one was open for 1% of the time, Pallas kernels for 4%

profile of v4, /device:TPU:1, one launch (start us, length us, event | category | flops | bytes accessed | tf_op | source)
XLA Modules:
  0.0 112.5 jit_solution(3038886668624151229)
XLA Ops:
  0.6 3.2 %shard_map.93 = bf16[8,528,256]{2,1,0:T(8,128)(2,1)} custom-call(bf16[128,2048]{1,0:T(8,128)(2,1)} %bitcast.15, bf16[128,2048]{1,0:T(8,128)(2,1)} %bitcast.16, bf16[128,2048]{1,0:T(8,128)(2,1)} %bitcast.17, bf16[128,2048]{1,0:T(8,128)(2,1)} %bitcast.18, f32[8,128]{1,0:T(8,128)} %bitcast.20), custom_call_target="tpu_custom_call" | custom-call | tf_op jit(solution)/shard_map/pallas_call | solution.py:44
  3.8 6.0 %all-to-all-start = ((bf16[8,528,256]{2,1,0:T(8,128)(2,1)}), bf16[8,528,256]{2,1,0:T(8,128)(2,1)S(1)}, u32[]{:S(2)}, u32[]{:S(2)}) async-start(bf16[8,528,256]{2,1,0:T(8,128)(2,1)} %shard_map.93), calls=%async_computation | async-start | bytes 4325376 | tf_op jit(solution)/shard_map/all_to_all | solution.py:305
  9.8 0.0 copy-start
  9.8 25.8 %all-to-all-done.got_ref = bf16[8,528,256]{2,1,0:T(8,128)(2,1)S(1)} async-done(((bf16[8,528,256]{2,1,0:T(8,128)(2,1)}), bf16[8,528,256]{2,1,0:T(8,128)(2,1)S(1)}, u32[]{:S(2)}, u32[]{:S(2)}) %all-to-all-start) | async-done | bytes 2162720 | tf_op jit(solution)/shard_map/all_to_all | solution.py:305
  35.6 1.9 %shard_map.94 = (bf16[256,256]{1,0:T(8,128)(2,1)}, f32[4,256,256]{2,1,0:T(8,128)S(1)}, f32[256,8]{1,0:T(8,128)S(1)}, f32[8,256]{1,0:T(8,128)S(1)}) custom-call(bf16[8,528,256]{2,1,0:T(8,128)(2,1)S(1)} %all-to-all-done.got_ref), custom_call_target="tpu_custom_call" | custom-call | tf_op jit(solution)/shard_map/pallas_call | solution.py:44
  37.5 5.4 %collective-permute-start = (bf16[256,256]{1,0:T(8,128)(2,1)}, bf16[256,256]{1,0:T(8,128)(2,1)S(1)}, u32[]{:S(2)}, u32[]{:S(2)}) collective-permute-start(bf16[256,256]{1,0:T(8,128)(2,1)} %get-tuple-element.21), channel_id=1, source_target_pairs={{0,8},{1,9},{2,10},{3,11},{4,12},{5,13},{6,14},{7,15},{8,0},{9,1},... | collective-permute-start | bytes 393224 | tf_op jit(solution)/shard_map/ppermute | solution.py:311
  42.8 0.1 pad_add_fusion.where_ref
  42.9 0.0 copy-done
  42.9 0.8 shard_map.95
  43.7 1.7 %collective-permute-done.middle_ref = bf16[256,256]{1,0:T(8,128)(2,1)S(1)} collective-permute-done((bf16[256,256]{1,0:T(8,128)(2,1)}, bf16[256,256]{1,0:T(8,128)(2,1)S(1)}, u32[]{:S(2)}, u32[]{:S(2)}) %collective-permute-start) | collective-permute-done | bytes 131104 | tf_op jit(solution)/shard_map/ppermute | solution.py:311
  45.4 4.9 %shard_map.96 = (bf16[8,384,256]{2,1,0:T(8,128)(2,1)}, bf16[256,256]{1,0:T(8,128)(2,1)}, f32[8,256]{1,0:T(8,128)S(1)}) custom-call(s32[2]{0:T(128)S(1)} %pad_add_fusion.where_ref, bf16[8,528,256]{2,1,0:T(8,128)(2,1)S(1)} %all-to-all-done.got_ref, f32[4,256,256]{2,1,0:T(8,128)S(1)} %get-tuple-element.16.states_ref, ...), custom_call_target="tpu_custom_call" | custom-call | tf_op jit(solution)/shard_map/pallas_call | solution.py:44
  50.3 5.2 %collective-permute-start.1 = (bf16[256,256]{1,0:T(8,128)(2,1)}, bf16[256,256]{1,0:T(8,128)(2,1)S(1)}, u32[]{:S(2)}, u32[]{:S(2)}) collective-permute-start(bf16[256,256]{1,0:T(8,128)(2,1)} %get-tuple-element.23), channel_id=1, source_target_pairs={{0,8},{1,9},{2,10},{3,11},{4,12},{5,13},{6,14},{7,15},{8,0},{9,1},... | collective-permute-start | bytes 393224 | tf_op jit(solution)/shard_map/ppermute | solution.py:327
  55.6 0.7 shard_map.99
  56.2 3.8 %all-to-all-start.2 = ((f32[16,8,256]{2,1,0:T(8,128)}), f32[16,8,256]{2,1,0:T(8,128)S(1)}, u32[]{:S(2)}, u32[]{:S(2)}) async-start(f32[16,8,256]{2,1,0:T(8,128)} %shard_map.99), calls=%async_computation.2 | async-start | bytes 262144 | tf_op jit(solution)/shard_map/all_to_all | solution.py:328
  60.0 0.0 collective-permute-done.1.middle_ref
  60.0 3.3 %shard_map.97 = bf16[8,384,256]{2,1,0:T(8,128)(2,1)} custom-call(s32[2]{0:T(128)S(1)} %pad_add_fusion.where_ref, bf16[8,528,256]{2,1,0:T(8,128)(2,1)S(1)} %all-to-all-done.got_ref, bf16[8,384,256]{2,1,0:T(8,128)(2,1)} %get-tuple-element.22.back_ref, bf16[256,256]{1,0:T(8,128)(2,1)S(1)} %collective-permute-done.1.middle_ref, ...), custom_call_target="tpu_custom_call", output_to_operand_aliasing={{}: (2, {})} | custom-call | tf_op jit(solution)/shard_map/pallas_call | solution.py:44
  63.4 3.4 %all-to-all-done.2 = f32[16,8,256]{2,1,0:T(8,128)S(1)} async-done(((f32[16,8,256]{2,1,0:T(8,128)}), f32[16,8,256]{2,1,0:T(8,128)S(1)}, u32[]{:S(2)}, u32[]{:S(2)}) %all-to-all-start.2) | async-done | bytes 131104 | tf_op jit(solution)/shard_map/all_to_all | solution.py:328
  66.8 3.6 %all-to-all-start.1 = ((bf16[8,384,256]{2,1,0:T(8,128)(2,1)}), bf16[8,384,256]{2,1,0:T(8,128)(2,1)S(1)}, u32[]{:S(2)}, u32[]{:S(2)}) async-start(bf16[8,384,256]{2,1,0:T(8,128)(2,1)} %shard_map.97), calls=%async_computation.1 | async-start | bytes 3145728 | tf_op jit(solution)/shard_map/all_to_all | solution.py:340
  70.4 40.2 %all-gather = f32[256,256]{1,0:T(8,128)S(1)} all-gather(f32[8,256]{1,0:T(8,128)S(1)} %reduce_sum.18), channel_id=2, replica_groups=mesh['dp'=32,'ctx'=16] {'dp'}, dimensions={0}, use_global_device_ids=true | all-gather | bytes 270336 | tf_op jit(solution)/shard_map/all_gather | solution.py:341
  110.6 0.6 copy.11
  111.2 0.0 all-to-all-done.1.got_ref
  111.2 1.3 %shard_map.98 = (bf16[128,2048]{1,0:T(8,128)(2,1)}, bf16[128,2048]{1,0:T(8,128)(2,1)}, bf16[128,2048]{1,0:T(8,128)(2,1)}) custom-call(bf16[8,384,256]{2,1,0:T(8,128)(2,1)S(1)} %all-to-all-done.1.got_ref), custom_call_target="tpu_custom_call" | custom-call | tf_op jit(solution)/shard_map/pallas_call | solution.py:44
  (5 shorter events, 0.1 us)
Async XLA Ops:
  3.8 31.8 %all-to-all-start = ((bf16[8,528,256]{2,1,0:T(8,128)(2,1)}), bf16[8,528,256]{2,1,0:T(8,128)(2,1)S(1)}, u32[]{:S(2)}, u32[]{:S(2)}) async-start(bf16[8,528,256]{2,1,0:T(8,128)(2,1)} %shard_map.93), calls=%async_computation | async-start | bytes 4325376 | tf_op jit(solution)/shard_map/all_to_all | solution.py:305
  9.8 33.2 %copy-start = (f32[2048]{0:T(1024)S(1)}, f32[2048]{0:T(1024)}, u32[]{:S(2)}) copy-start(f32[2048]{0:T(1024)} %param.11) | copy-start | bytes 24580
  37.5 7.9 %collective-permute-start = (bf16[256,256]{1,0:T(8,128)(2,1)}, bf16[256,256]{1,0:T(8,128)(2,1)S(1)}, u32[]{:S(2)}, u32[]{:S(2)}) collective-permute-start(bf16[256,256]{1,0:T(8,128)(2,1)} %get-tuple-element.21), channel_id=1, source_target_pairs={{0,8},{1,9},{2,10},{3,11},{4,12},{5,13},{6,14},{7,15},{8,0},{9,1},... | collective-permute-start | bytes 393224 | tf_op jit(solution)/shard_map/ppermute | solution.py:311
  50.3 9.7 %collective-permute-start.1 = (bf16[256,256]{1,0:T(8,128)(2,1)}, bf16[256,256]{1,0:T(8,128)(2,1)S(1)}, u32[]{:S(2)}, u32[]{:S(2)}) collective-permute-start(bf16[256,256]{1,0:T(8,128)(2,1)} %get-tuple-element.23), channel_id=1, source_target_pairs={{0,8},{1,9},{2,10},{3,11},{4,12},{5,13},{6,14},{7,15},{8,0},{9,1},... | collective-permute-start | bytes 393224 | tf_op jit(solution)/shard_map/ppermute | solution.py:327
  56.2 10.5 %all-to-all-start.2 = ((f32[16,8,256]{2,1,0:T(8,128)}), f32[16,8,256]{2,1,0:T(8,128)S(1)}, u32[]{:S(2)}, u32[]{:S(2)}) async-start(f32[16,8,256]{2,1,0:T(8,128)} %shard_map.99), calls=%async_computation.2 | async-start | bytes 262144 | tf_op jit(solution)/shard_map/all_to_all | solution.py:328
  66.8 44.4 %all-to-all-start.1 = ((bf16[8,384,256]{2,1,0:T(8,128)(2,1)}), bf16[8,384,256]{2,1,0:T(8,128)(2,1)S(1)}, u32[]{:S(2)}, u32[]{:S(2)}) async-start(bf16[8,384,256]{2,1,0:T(8,128)(2,1)} %shard_map.97), calls=%async_computation.1 | async-start | bytes 3145728 | tf_op jit(solution)/shard_map/all_to_all | solution.py:340

commit v5 on v4

--- a/solution.py
+++ b/solution.py
@@ -338,7 +338,8 @@
         aliases={2: 0},
     )(where, got, back, middle_grad, column, line)[0]
     back = lax.all_to_all(back, "ctx", 0, 0, axis_index_groups=halves, tiled=True)
-    gain_all = lax.all_gather(jnp.sum(gains, axis=0), "dp")
+    gain_rows = jnp.pad(jnp.sum(gains, axis=0), ((0, 24), (0, 0)))
+    gain_all = lax.all_gather(gain_rows, "dp")[:, :HEADS]
     results = call(
         unpack_kernel,
         [((TOK, HEADS * KD), BF16)] * 3,

time: 113 us -> 154 us (1.36)
  waiting for transfers between devices: 30.9 us -> 73.9 us
  between operations: 0.75 us -> 14.1 us
  starting transfers between devices: 23.9 us -> 14.2 us
  blocking collectives: 40.2 us -> 33.3 us
    all_gather x0 -> x1, waiting for transfers between devices: none -> 42.1 us  [shards(): gain_all = lax.all_gather(gain_rows, 'dp')[:, :HEADS]]
    all_gather x1 -> x0, blocking collectives: 40.2 us -> none  [shards(): gain_all = lax.all_gather(jnp.sum(gains, axis=0), 'dp')]
    all_to_all x0 -> x2, blocking collectives: none -> 33.3 us  [the longest x1 20.4 us: shards(): lax.all_to_all(back, 'ctx', 0, 0, axis_index_groups=halves, tiled=True)]
    all_to_all x2 -> x0, starting transfers between devices: 7.37 us -> none  [the longest x1 3.79 us: shards(): lax.all_to_all(call(spread_kernel, [((blocks, HEADS, VD), F32)], cost=(4...]
    ppermute x1, waiting for transfers between devices: 0.01 us -> 4.32 us  [shards(): middle_grad = lax.ppermute(total_grad, 'ctx', swap)]
    all_to_all x2 -> x0, waiting for transfers between devices: 3.41 us -> none  [the longest x1 3.4 us: shards(): lax.all_to_all(call(spread_kernel, [((blocks, HEADS, VD), F32)], cost=(4...]
    ppermute x1, starting transfers between devices: 5.21 us -> 2.89 us  [shards(): middle_grad = lax.ppermute(total_grad, 'ctx', swap)]
  transfers between devices with their start and end apart: 5 -> 4, of which waited for: 3 -> 4; matrix products, arithmetic and copies ran while one was open for 1% -> 0% of each run, Pallas kernels for 4% -> 4%
where the time goes in v5:
time: 154 us; the launch traced here: 153 us
  waiting for transfers between devices  73.9 us (48%)
  blocking collectives  33.3 us (22%)
  Pallas kernels  15.4 us (10%)
  starting transfers between devices  14.2 us (9%)
  between operations  14.1 us (9%)
    all_gather x1, waiting for transfers between devices, shards(): gain_all = lax.all_gather(gain_rows, 'dp')[:, :HEADS]  42.1 us
    all_to_all x1, waiting for transfers between devices, shards(): lax.all_to_all(packed, 'ctx', 0, 0, axis_index_groups=halves, tiled=True)  25.8 us
    all_to_all x1, blocking collectives, shards(): lax.all_to_all(back, 'ctx', 0, 0, axis_index_groups=halves, tiled=True)  20.4 us
    pallas_call x7, Pallas kernels, run(): pl.pallas_call(kernel, out_shape=[(pltpu.HBM if i in far else jax.ShapeDt...  15.4 us
    all_to_all x1, blocking collectives, shards(): lax.all_to_all(call(spread_kernel, [((blocks, HEADS, VD), F32)], cost=(4...  13 us
    all_to_all x1, starting transfers between devices, shards(): lax.all_to_all(packed, 'ctx', 0, 0, axis_index_groups=halves, tiled=True)  5.96 us
    ppermute x1, starting transfers between devices, shards(): middle = lax.ppermute(total, 'ctx', swap)  5.36 us
    ppermute x1, waiting for transfers between devices, shards(): middle_grad = lax.ppermute(total_grad, 'ctx', swap)  4.32 us
  transfers between devices with their start and end apart: 4, of which 4 were waited for; matrix products, arithmetic and copies ran while one was open for 0% of the time, Pallas kernels for 4%

profile of v5, /device:TPU:1, one launch (start us, length us, event | category | flops | bytes accessed | tf_op | source)
XLA Modules:
  0.0 153.3 jit_solution(7692150703616374150)
XLA Ops:
  7.2 3.2 %shard_map.93 = bf16[8,528,256]{2,1,0:T(8,128)(2,1)} custom-call(bf16[128,2048]{1,0:T(8,128)(2,1)} %bitcast.14, bf16[128,2048]{1,0:T(8,128)(2,1)} %bitcast.15, bf16[128,2048]{1,0:T(8,128)(2,1)} %bitcast.16, bf16[128,2048]{1,0:T(8,128)(2,1)} %bitcast.17, f32[8,128]{1,0:T(8,128)} %bitcast.20), custom_call_target="tpu_custom_call" | custom-call | tf_op jit(solution)/shard_map/pallas_call | solution.py:44
  10.3 6.0 %all-to-all-start = ((bf16[8,528,256]{2,1,0:T(8,128)(2,1)}), bf16[8,528,256]{2,1,0:T(8,128)(2,1)S(1)}, u32[]{:S(2)}, u32[]{:S(2)}) async-start(bf16[8,528,256]{2,1,0:T(8,128)(2,1)} %shard_map.93), calls=%async_computation | async-start | bytes 4325376 | tf_op jit(solution)/shard_map/all_to_all | solution.py:305
  16.3 0.0 copy-start
  16.3 0.0 all-gather.3.cloned.1.call-start
  16.4 25.8 %all-to-all-done.got_ref = bf16[8,528,256]{2,1,0:T(8,128)(2,1)S(1)} async-done(((bf16[8,528,256]{2,1,0:T(8,128)(2,1)}), bf16[8,528,256]{2,1,0:T(8,128)(2,1)S(1)}, u32[]{:S(2)}, u32[]{:S(2)}) %all-to-all-start) | async-done | bytes 2162720 | tf_op jit(solution)/shard_map/all_to_all | solution.py:305
  42.1 1.9 %shard_map.94 = (bf16[256,256]{1,0:T(8,128)(2,1)}, f32[4,256,256]{2,1,0:T(8,128)S(1)}, f32[256,8]{1,0:T(8,128)S(1)}, f32[8,256]{1,0:T(8,128)S(1)}) custom-call(bf16[8,528,256]{2,1,0:T(8,128)(2,1)S(1)} %all-to-all-done.got_ref), custom_call_target="tpu_custom_call" | custom-call | tf_op jit(solution)/shard_map/pallas_call | solution.py:44
  44.0 5.4 %collective-permute-start = (bf16[256,256]{1,0:T(8,128)(2,1)}, bf16[256,256]{1,0:T(8,128)(2,1)S(1)}, u32[]{:S(2)}, u32[]{:S(2)}) collective-permute-start(bf16[256,256]{1,0:T(8,128)(2,1)} %get-tuple-element.21), channel_id=1, source_target_pairs={{0,8},{1,9},{2,10},{3,11},{4,12},{5,13},{6,14},{7,15},{8,0},{9,1},... | collective-permute-start | bytes 393224 | tf_op jit(solution)/shard_map/ppermute | solution.py:311
  49.4 0.1 pad_add_fusion.where_ref
  49.5 0.0 copy-done
  49.5 0.8 shard_map.95
  50.2 1.7 %collective-permute-done.middle_ref = bf16[256,256]{1,0:T(8,128)(2,1)S(1)} collective-permute-done((bf16[256,256]{1,0:T(8,128)(2,1)}, bf16[256,256]{1,0:T(8,128)(2,1)S(1)}, u32[]{:S(2)}, u32[]{:S(2)}) %collective-permute-start) | collective-permute-done | bytes 131104 | tf_op jit(solution)/shard_map/ppermute | solution.py:311
  51.9 4.9 %shard_map.96 = (bf16[8,384,256]{2,1,0:T(8,128)(2,1)}, bf16[256,256]{1,0:T(8,128)(2,1)}, f32[8,256]{1,0:T(8,128)S(1)}) custom-call(s32[2]{0:T(128)S(1)} %pad_add_fusion.where_ref, bf16[8,528,256]{2,1,0:T(8,128)(2,1)S(1)} %all-to-all-done.got_ref, f32[4,256,256]{2,1,0:T(8,128)S(1)} %get-tuple-element.16.states_ref, ...), custom_call_target="tpu_custom_call" | custom-call | tf_op jit(solution)/shard_map/pallas_call | solution.py:44
  56.9 0.0 copy-start.1
  56.9 13.0 %all_to_all.15 = f32[16,8,256]{2,1,0:T(8,128)S(1)} all-to-all(f32[16,8,256]{2,1,0:T(8,128)S(1)} %shard_map.99), channel_id=1, replica_groups=mesh['dp'=32,'ctx'=16] {'ctx'}, dimensions={0} | all-to-all | bytes 262144 | tf_op jit(solution)/shard_map/all_to_all | solution.py:328
  69.9 0.6 pad.4
  70.5 0.0 all-gather.3.cloned.1.call-update
  70.5 0.0 copy-done.1
  70.5 2.9 %collective-permute-start.1 = (bf16[256,256]{1,0:T(8,128)(2,1)S(1)}, bf16[256,256]{1,0:T(8,128)(2,1)S(1)}, u32[]{:S(2)}, u32[]{:S(2)}) collective-permute-start(bf16[256,256]{1,0:T(8,128)(2,1)S(1)} %copy-done.1), channel_id=1, source_target_pairs={{0,8},{1,9},{2,10},{3,11},{4,12},{5,13},{6,14},{7,15},{8,0},{9,1},... | collective-permute-start | bytes 393224 | tf_op jit(solution)/shard_map/ppermute | solution.py:327
  73.4 4.3 %collective-permute-done.1.middle_ref = bf16[256,256]{1,0:T(8,128)(2,1)S(1)} collective-permute-done((bf16[256,256]{1,0:T(8,128)(2,1)S(1)}, bf16[256,256]{1,0:T(8,128)(2,1)S(1)}, u32[]{:S(2)}, u32[]{:S(2)}) %collective-permute-start.1) | collective-permute-done | bytes 131104 | tf_op jit(solution)/shard_map/ppermute | solution.py:327
  77.7 3.3 %shard_map.97 = bf16[8,384,256]{2,1,0:T(8,128)(2,1)} custom-call(s32[2]{0:T(128)S(1)} %pad_add_fusion.where_ref, bf16[8,528,256]{2,1,0:T(8,128)(2,1)S(1)} %all-to-all-done.got_ref, bf16[8,384,256]{2,1,0:T(8,128)(2,1)} %get-tuple-element.22.back_ref, bf16[256,256]{1,0:T(8,128)(2,1)S(1)} %collective-permute-done.1.middle_ref, ...), custom_call_target="tpu_custom_call", output_to_operand_aliasing={{}: (2, {})} | custom-call | tf_op jit(solution)/shard_map/pallas_call | solution.py:44
  81.1 20.4 %all_to_all.16.got_ref = bf16[8,384,256]{2,1,0:T(8,128)(2,1)S(1)} all-to-all(bf16[8,384,256]{2,1,0:T(8,128)(2,1)} %shard_map.97), channel_id=1, replica_groups={{0,1,2,3,4,5,6,7},{8,9,10,11,12,13,14,15},{16,17,18,19,20,21,22,23},{24..., dimensions={0} | all-to-all | bytes 3145728 | tf_op jit(solution)/shard_map/all_to_all | solution.py:340
  101.4 1.3 shard_map.98
  102.8 42.1 %all-gather.3.cloned.1.call-done = f32[1024,256]{1,0:T(8,128)} async-done(((f32[32,256]{1,0:T(8,128)}), f32[1024,256]{1,0:T(8,128)}) %all-gather.3.cloned.1.call-update) | async-done | bytes 1048592 | tf_op jit(solution)/shard_map/all_gather | solution.py:342
  144.9 1.0 slice_reduce_fusion
  145.9 0.6 copy.11
  (5 shorter events, 0.0 us)
Async XLA Ops:
  10.3 31.8 %all-to-all-start = ((bf16[8,528,256]{2,1,0:T(8,128)(2,1)}), bf16[8,528,256]{2,1,0:T(8,128)(2,1)S(1)}, u32[]{:S(2)}, u32[]{:S(2)}) async-start(bf16[8,528,256]{2,1,0:T(8,128)(2,1)} %shard_map.93), calls=%async_computation | async-start | bytes 4325376 | tf_op jit(solution)/shard_map/all_to_all | solution.py:305
  16.3 33.2 %copy-start = (f32[2048]{0:T(1024)S(1)}, f32[2048]{0:T(1024)}, u32[]{:S(2)}) copy-start(f32[2048]{0:T(1024)} %param.11) | copy-start | bytes 24580
  16.3 128.6 %all-gather.3.cloned.1.call-start = ((), (), s32[]{:S(2)}) async-start(), calls=%async_computation.3 | async-start | bytes 1081344 | tf_op jit(solution)/shard_map/all_gather | solution.py:342
  44.0 7.9 %collective-permute-start = (bf16[256,256]{1,0:T(8,128)(2,1)}, bf16[256,256]{1,0:T(8,128)(2,1)S(1)}, u32[]{:S(2)}, u32[]{:S(2)}) collective-permute-start(bf16[256,256]{1,0:T(8,128)(2,1)} %get-tuple-element.21), channel_id=1, source_target_pairs={{0,8},{1,9},{2,10},{3,11},{4,12},{5,13},{6,14},{7,15},{8,0},{9,1},... | collective-permute-start | bytes 393224 | tf_op jit(solution)/shard_map/ppermute | solution.py:311
  56.9 13.6 %copy-start.1 = (bf16[256,256]{1,0:T(8,128)(2,1)S(1)}, bf16[256,256]{1,0:T(8,128)(2,1)}, u32[]{:S(2)}) copy-start(bf16[256,256]{1,0:T(8,128)(2,1)} %get-tuple-element.23) | copy-start | bytes 393220
  70.5 7.2 %collective-permute-start.1 = (bf16[256,256]{1,0:T(8,128)(2,1)S(1)}, bf16[256,256]{1,0:T(8,128)(2,1)S(1)}, u32[]{:S(2)}, u32[]{:S(2)}) collective-permute-start(bf16[256,256]{1,0:T(8,128)(2,1)S(1)} %copy-done.1), channel_id=1, source_target_pairs={{0,8},{1,9},{2,10},{3,11},{4,12},{5,13},{6,14},{7,15},{8,0},{9,1},... | collective-permute-start | bytes 393224 | tf_op jit(solution)/shard_map/ppermute | solution.py:327
Sparse Core Ops, SparseCore 0:
  70.6 74.1 all-gather.2

commit v6 on v4

--- a/solution.py
+++ b/solution.py
@@ -338,7 +338,11 @@
         aliases={2: 0},
     )(where, got, back, middle_grad, column, line)[0]
     back = lax.all_to_all(back, "ctx", 0, 0, axis_index_groups=halves, tiled=True)
-    gain_all = lax.all_gather(jnp.sum(gains, axis=0), "dp")
+    gain_sum = jnp.sum(gains, axis=0)
+    near = [list(range(i, i + 8)) for i in range(0, size, 8)]
+    apart = [list(range(i, size, 8)) for i in range(8)]
+    for groups in (near, apart):
+        gain_sum = jnp.sum(lax.all_gather(gain_sum, "dp", axis_index_groups=groups), axis=0)
     results = call(
         unpack_kernel,
         [((TOK, HEADS * KD), BF16)] * 3,
@@ -346,7 +350,7 @@
         places={0: pl.ANY},
         far=(0, 1, 2),
     )(back)
-    grad_gain = (jnp.sum(gain_all, axis=0) / size).reshape(HEADS * VD)
+    grad_gain = (gain_sum / size).reshape(HEADS * VD)
     return (*(item[None] for item in results), grad_gain)
 
 

time: 113 us -> 115 us (1.018)
  the two profiles are of different devices: /device:TPU:1 before, /device:TPU:2 now
where the time goes in v6:
time: 115 us; the launch traced here: 114 us
  blocking collectives  39.9 us (35%)
  waiting for transfers between devices  29.4 us (26%)
  starting transfers between devices  27.6 us (24%)
  Pallas kernels  16.1 us (14%)
    all_gather x2, blocking collectives, shards(): lax.all_gather(gain_sum, 'dp', axis_index_groups=groups)  39.9 us
    all_to_all x1, waiting for transfers between devices, shards(): lax.all_to_all(packed, 'ctx', 0, 0, axis_index_groups=halves, tiled=True)  22.7 us
    pallas_call x7, Pallas kernels, run(): pl.pallas_call(kernel, out_shape=[(pltpu.HBM if i in far else jax.ShapeDt...  16.1 us
    all_to_all x1, starting transfers between devices, shards(): lax.all_to_all(packed, 'ctx', 0, 0, axis_index_groups=halves, tiled=True)  9.45 us
    all_to_all x1, starting transfers between devices, shards(): lax.all_to_all(back, 'ctx', 0, 0, axis_index_groups=halves, tiled=True)  5.05 us
    all_to_all x1, starting transfers between devices, shards(): lax.all_to_all(call(spread_kernel, [((blocks, HEADS, VD), F32)], cost=(4...  4.94 us
    ppermute x1, starting transfers between devices, shards(): middle_grad = lax.ppermute(total_grad, 'ctx', swap)  4.15 us
    ppermute x1, starting transfers between devices, shards(): middle = lax.ppermute(total, 'ctx', swap)  4.02 us
  transfers between devices with their start and end apart: 5, of which 3 were waited for; matrix products, arithmetic and copies ran while one was open for 1% of the time, Pallas kernels for 4%

profile of v6, /device:TPU:2, one launch (start us, length us, event | category | flops | bytes accessed | tf_op | source)
XLA Modules:
  0.0 114.5 jit_solution(14837539799308939855)
XLA Ops:
  0.6 3.2 %shard_map.93 = bf16[8,528,256]{2,1,0:T(8,128)(2,1)} custom-call(bf16[128,2048]{1,0:T(8,128)(2,1)} %bitcast.17, bf16[128,2048]{1,0:T(8,128)(2,1)} %bitcast.18, bf16[128,2048]{1,0:T(8,128)(2,1)} %bitcast.19, bf16[128,2048]{1,0:T(8,128)(2,1)} %bitcast.20, f32[8,128]{1,0:T(8,128)} %bitcast.22), custom_call_target="tpu_custom_call" | custom-call | tf_op jit(solution)/shard_map/pallas_call | solution.py:44
  3.8 9.4 %all-to-all-start = ((bf16[8,528,256]{2,1,0:T(8,128)(2,1)}), bf16[8,528,256]{2,1,0:T(8,128)(2,1)S(1)}, u32[]{:S(2)}, u32[]{:S(2)}) async-start(bf16[8,528,256]{2,1,0:T(8,128)(2,1)} %shard_map.93), calls=%async_computation | async-start | bytes 4325376 | tf_op jit(solution)/shard_map/all_to_all | solution.py:305
  13.3 0.0 copy-start
  13.3 22.7 %all-to-all-done.got_ref = bf16[8,528,256]{2,1,0:T(8,128)(2,1)S(1)} async-done(((bf16[8,528,256]{2,1,0:T(8,128)(2,1)}), bf16[8,528,256]{2,1,0:T(8,128)(2,1)S(1)}, u32[]{:S(2)}, u32[]{:S(2)}) %all-to-all-start) | async-done | bytes 2162720 | tf_op jit(solution)/shard_map/all_to_all | solution.py:305
  35.9 1.9 %shard_map.94 = (bf16[256,256]{1,0:T(8,128)(2,1)}, f32[4,256,256]{2,1,0:T(8,128)S(1)}, f32[256,8]{1,0:T(8,128)S(1)}, f32[8,256]{1,0:T(8,128)S(1)}) custom-call(bf16[8,528,256]{2,1,0:T(8,128)(2,1)S(1)} %all-to-all-done.got_ref), custom_call_target="tpu_custom_call" | custom-call | tf_op jit(solution)/shard_map/pallas_call | solution.py:44
  37.8 4.0 %collective-permute-start = (bf16[256,256]{1,0:T(8,128)(2,1)}, bf16[256,256]{1,0:T(8,128)(2,1)S(1)}, u32[]{:S(2)}, u32[]{:S(2)}) collective-permute-start(bf16[256,256]{1,0:T(8,128)(2,1)} %get-tuple-element.21), channel_id=1, source_target_pairs={{0,8},{1,9},{2,10},{3,11},{4,12},{5,13},{6,14},{7,15},{8,0},{9,1},... | collective-permute-start | bytes 393224 | tf_op jit(solution)/shard_map/ppermute | solution.py:311
  41.8 0.1 pad_add_fusion.where_ref
  41.9 0.0 copy-done
  41.9 0.8 shard_map.95
  42.7 3.7 %collective-permute-done.middle_ref = bf16[256,256]{1,0:T(8,128)(2,1)S(1)} collective-permute-done((bf16[256,256]{1,0:T(8,128)(2,1)}, bf16[256,256]{1,0:T(8,128)(2,1)S(1)}, u32[]{:S(2)}, u32[]{:S(2)}) %collective-permute-start) | collective-permute-done | bytes 131104 | tf_op jit(solution)/shard_map/ppermute | solution.py:311
  46.4 4.9 %shard_map.96 = (bf16[8,384,256]{2,1,0:T(8,128)(2,1)}, bf16[256,256]{1,0:T(8,128)(2,1)}, f32[8,256]{1,0:T(8,128)S(1)}) custom-call(s32[2]{0:T(128)S(1)} %pad_add_fusion.where_ref, bf16[8,528,256]{2,1,0:T(8,128)(2,1)S(1)} %all-to-all-done.got_ref, f32[4,256,256]{2,1,0:T(8,128)S(1)} %get-tuple-element.16.states_ref, ...), custom_call_target="tpu_custom_call" | custom-call | tf_op jit(solution)/shard_map/pallas_call | solution.py:44
  51.3 4.1 %collective-permute-start.1 = (bf16[256,256]{1,0:T(8,128)(2,1)}, bf16[256,256]{1,0:T(8,128)(2,1)S(1)}, u32[]{:S(2)}, u32[]{:S(2)}) collective-permute-start(bf16[256,256]{1,0:T(8,128)(2,1)} %get-tuple-element.23), channel_id=1, source_target_pairs={{0,8},{1,9},{2,10},{3,11},{4,12},{5,13},{6,14},{7,15},{8,0},{9,1},... | collective-permute-start | bytes 393224 | tf_op jit(solution)/shard_map/ppermute | solution.py:327
  55.5 0.7 shard_map.99
  56.1 4.9 %all-to-all-start.2 = ((f32[16,8,256]{2,1,0:T(8,128)}), f32[16,8,256]{2,1,0:T(8,128)S(1)}, u32[]{:S(2)}, u32[]{:S(2)}) async-start(f32[16,8,256]{2,1,0:T(8,128)} %shard_map.99), calls=%async_computation.2 | async-start | bytes 262144 | tf_op jit(solution)/shard_map/all_to_all | solution.py:328
  61.1 0.0 collective-permute-done.1.middle_ref
  61.1 3.3 %shard_map.97 = bf16[8,384,256]{2,1,0:T(8,128)(2,1)} custom-call(s32[2]{0:T(128)S(1)} %pad_add_fusion.where_ref, bf16[8,528,256]{2,1,0:T(8,128)(2,1)S(1)} %all-to-all-done.got_ref, bf16[8,384,256]{2,1,0:T(8,128)(2,1)} %get-tuple-element.22.back_ref, bf16[256,256]{1,0:T(8,128)(2,1)S(1)} %collective-permute-done.1.middle_ref, ...), custom_call_target="tpu_custom_call", output_to_operand_aliasing={{}: (2, {})} | custom-call | tf_op jit(solution)/shard_map/pallas_call | solution.py:44
  64.4 3.1 %all-to-all-done.2 = f32[16,8,256]{2,1,0:T(8,128)S(1)} async-done(((f32[16,8,256]{2,1,0:T(8,128)}), f32[16,8,256]{2,1,0:T(8,128)S(1)}, u32[]{:S(2)}, u32[]{:S(2)}) %all-to-all-start.2) | async-done | bytes 131104 | tf_op jit(solution)/shard_map/all_to_all | solution.py:328
  67.5 5.0 %all-to-all-start.1 = ((bf16[8,384,256]{2,1,0:T(8,128)(2,1)}), bf16[8,384,256]{2,1,0:T(8,128)(2,1)S(1)}, u32[]{:S(2)}, u32[]{:S(2)}) async-start(bf16[8,384,256]{2,1,0:T(8,128)(2,1)} %shard_map.97), calls=%async_computation.1 | async-start | bytes 3145728 | tf_op jit(solution)/shard_map/all_to_all | solution.py:340
  72.6 15.0 %all-gather = f32[64,256]{1,0:T(8,128)S(1)} all-gather(f32[8,256]{1,0:T(8,128)S(1)} %reduce_sum.27), channel_id=2, replica_groups={{0,16,32,48,64,80,96,112},{128,144,160,176,192,208,224,240},{256,272,28..., dimensions={0}, use_global_device_ids=true | all-gather | bytes 73728 | tf_op jit(solution)/shard_map/all_gather | solution.py:345
  87.6 24.9 %all-gather.1 = f32[32,256]{1,0:T(8,128)S(1)} all-gather(f32[8,256]{1,0:T(8,128)S(1)} %bitcast_reduce_fusion), channel_id=3, replica_groups={{0,128,256,384},{16,144,272,400},{32,160,288,416},{48,176,304,432},{64,..., dimensions={0}, use_global_device_ids=true | all-gather | bytes 40960 | tf_op jit(solution)/shard_map/all_gather | solution.py:345
  112.5 0.6 copy.11
  113.1 0.0 all-to-all-done.1.got_ref
  113.1 1.3 %shard_map.98 = (bf16[128,2048]{1,0:T(8,128)(2,1)}, bf16[128,2048]{1,0:T(8,128)(2,1)}, bf16[128,2048]{1,0:T(8,128)(2,1)}) custom-call(bf16[8,384,256]{2,1,0:T(8,128)(2,1)S(1)} %all-to-all-done.1.got_ref), custom_call_target="tpu_custom_call" | custom-call | tf_op jit(solution)/shard_map/pallas_call | solution.py:44
  (6 shorter events, 0.1 us)
Async XLA Ops:
  3.8 32.1 %all-to-all-start = ((bf16[8,528,256]{2,1,0:T(8,128)(2,1)}), bf16[8,528,256]{2,1,0:T(8,128)(2,1)S(1)}, u32[]{:S(2)}, u32[]{:S(2)}) async-start(bf16[8,528,256]{2,1,0:T(8,128)(2,1)} %shard_map.93), calls=%async_computation | async-start | bytes 4325376 | tf_op jit(solution)/shard_map/all_to_all | solution.py:305
  13.3 28.7 %copy-start = (f32[2048]{0:T(1024)S(1)}, f32[2048]{0:T(1024)}, u32[]{:S(2)}) copy-start(f32[2048]{0:T(1024)} %param.11) | copy-start | bytes 24580
  37.8 8.6 %collective-permute-start = (bf16[256,256]{1,0:T(8,128)(2,1)}, bf16[256,256]{1,0:T(8,128)(2,1)S(1)}, u32[]{:S(2)}, u32[]{:S(2)}) collective-permute-start(bf16[256,256]{1,0:T(8,128)(2,1)} %get-tuple-element.21), channel_id=1, source_target_pairs={{0,8},{1,9},{2,10},{3,11},{4,12},{5,13},{6,14},{7,15},{8,0},{9,1},... | collective-permute-start | bytes 393224 | tf_op jit(solution)/shard_map/ppermute | solution.py:311
  51.3 9.8 %collective-permute-start.1 = (bf16[256,256]{1,0:T(8,128)(2,1)}, bf16[256,256]{1,0:T(8,128)(2,1)S(1)}, u32[]{:S(2)}, u32[]{:S(2)}) collective-permute-start(bf16[256,256]{1,0:T(8,128)(2,1)} %get-tuple-element.23), channel_id=1, source_target_pairs={{0,8},{1,9},{2,10},{3,11},{4,12},{5,13},{6,14},{7,15},{8,0},{9,1},... | collective-permute-start | bytes 393224 | tf_op jit(solution)/shard_map/ppermute | solution.py:327
  56.1 11.3 %all-to-all-start.2 = ((f32[16,8,256]{2,1,0:T(8,128)}), f32[16,8,256]{2,1,0:T(8,128)S(1)}, u32[]{:S(2)}, u32[]{:S(2)}) async-start(f32[16,8,256]{2,1,0:T(8,128)} %shard_map.99), calls=%async_computation.2 | async-start | bytes 262144 | tf_op jit(solution)/shard_map/all_to_all | solution.py:328
  67.5 45.6 %all-to-all-start.1 = ((bf16[8,384,256]{2,1,0:T(8,128)(2,1)}), bf16[8,384,256]{2,1,0:T(8,128)(2,1)S(1)}, u32[]{:S(2)}, u32[]{:S(2)}) async-start(bf16[8,384,256]{2,1,0:T(8,128)(2,1)} %shard_map.97), calls=%async_computation.1 | async-start | bytes 3145728 | tf_op jit(solution)/shard_map/all_to_all | solution.py:340

commit v7 on v4

--- a/solution.py
+++ b/solution.py
@@ -141,16 +141,17 @@
     decay_ref[...] = jnp.zeros_like(decay_ref)
     for i in range(GROUP):
         pieces = got_ref[i, 4 * TOK :, :].astype(F32)
-        decay = pieces[0:1, :TOK] + pieces[0:1, TOK:] + pieces[1:2, :TOK]
         c, j = divmod(i * TOK, CHUNK)
-        decay_ref[c : c + 1, j : j + TOK] = decay
-    decay = decay_ref[...]
+        for n, piece in enumerate((pieces[0:1, :TOK], pieces[0:1, TOK:], pieces[1:2, :TOK])):
+            decay_ref[8 * n + c : 8 * n + c + 1, j : j + TOK] = piece
+    pieces = decay_ref[...].astype(BF16)
     t = lax.broadcasted_iota(jnp.int32, (CHUNK, CHUNK), 0)
     s = lax.broadcasted_iota(jnp.int32, (CHUNK, CHUNK), 1)
-    lower = (t >= s).astype(F32)
-    exact = dict(precision=lax.Precision.HIGHEST, preferred_element_type=F32)
-    row_ref[...] = lax.dot_general(decay, lower, (((1,), (1,)), ((), ())), **exact)
-    col_ref[...] = lax.dot_general(lower, decay, (((1,), (1,)), ((), ())), **exact)
+    lower = (t >= s).astype(F32).astype(BF16)
+    lines = nt(pieces, lower)
+    row_ref[...] = (lines[0:8] + lines[8:16]) + lines[16:24]
+    columns = nt(lower, pieces)
+    col_ref[...] = (columns[:, 0:8] + columns[:, 8:16]) + columns[:, 16:24]
     carried = jnp.zeros((KD, VD), F32)
     for c in range(CHUNKS):
         states_ref[c] = carried
@@ -229,8 +230,9 @@
     total_buf[...] = carried.astype(BF16)
     copies.append(pltpu.make_async_copy(total_buf, total_ref, sems.at[3, 0]))
     copies[-1].start()
-    mine = lax.broadcasted_iota(jnp.int32, (HEADS, VD), 0) == where_ref[1]
-    gain_part_ref[...] = jnp.where(mine, gain_part, 0.0)
+    gain_part_ref[...] = jnp.zeros_like(gain_part_ref)
+    gain_part_ref[0:1, :] = gain_part[:, :128]
+    gain_part_ref[1:2, :] = gain_part[:, 128:]
     for copy in copies:
         copy.wait()
 
@@ -238,6 +240,13 @@
 def spread_kernel(gain_ref, out_ref):
     for i in range(out_ref.shape[0]):
         out_ref[i] = gain_ref[...]
+
+
+def fold_kernel(gains_ref, out_ref):
+    for h in range(HEADS):
+        for j in range(2):
+            both = gains_ref[h, j : j + 1, :] + gains_ref[h + GROUP, j : j + 1, :]
+            out_ref[2 * h + j : 2 * h + j + 1, :] = both
 
 
 def last_kernel(where_ref, got_ref, back_ref, middle_ref, col_ref, row_ref, out_ref, buf, sems, out_sems):
@@ -285,8 +294,6 @@
     halves = [list(range(GROUP)), list(range(GROUP, 2 * GROUP))]
     size = lax.axis_size("dp")
     swap = [(i, i ^ GROUP) for i in range(blocks)]
-    where = jnp.stack([place // GROUP, place % GROUP]).astype(jnp.int32)
-    gain = lax.dynamic_slice_in_dim(norm_gain.reshape(HEADS, VD), place % GROUP, 1, 0)
     square = (CHUNKS, CHUNK, 256)
 
     packed = call(
@@ -303,10 +310,12 @@
         far=(0,),
     )(queries[0], key_vectors[0], values[0], grad_out[0], log_decay[0])[0]
     got = lax.all_to_all(packed, "ctx", 0, 0, axis_index_groups=halves, tiled=True)
+    where = (place // GROUP).astype(jnp.int32).reshape(1)
+    gain = lax.dynamic_slice_in_dim(norm_gain.reshape(HEADS, VD), place % GROUP, 1, 0)
     total, states, column, line = call(
         state_kernel,
         [((KD, VD), BF16), ((CHUNKS, KD, VD), F32), ((CHUNK, 8), F32), ((8, CHUNK), F32)],
-        [pltpu.VMEM((8, CHUNK), F32)],
+        [pltpu.VMEM((32, CHUNK), F32)],
     )(got)
     middle = lax.ppermute(total, "ctx", swap)
     retained, output = call(local_kernel, [(square, BF16), (square, F32)])(
@@ -314,7 +323,7 @@
     )
     back, total_grad, gain_part = call(
         output_kernel,
-        [((GROUP, BACK, 256), BF16), ((KD, VD), BF16), ((HEADS, VD), F32)],
+        [((GROUP, BACK, 256), BF16), ((KD, VD), BF16), ((8, 128), F32)],
         [
             pltpu.VMEM((GROUP, BACK, 256), BF16),
             pltpu.VMEM((KD, VD), BF16),
@@ -326,7 +335,7 @@
     )(where, got, states, retained, output, middle, column, line, gain)
     middle_grad = lax.ppermute(total_grad, "ctx", swap)
     gains = lax.all_to_all(
-        call(spread_kernel, [((blocks, HEADS, VD), F32)], cost=(4 * 10**9, 2**20))(gain_part)[0],
+        call(spread_kernel, [((blocks, 8, 128), F32)], cost=(4 * 10**9, 2**20))(gain_part)[0],
         "ctx", 0, 0, tiled=True,
     )
     back = call(
@@ -338,7 +347,7 @@
         aliases={2: 0},
     )(where, got, back, middle_grad, column, line)[0]
     back = lax.all_to_all(back, "ctx", 0, 0, axis_index_groups=halves, tiled=True)
-    gain_all = lax.all_gather(jnp.sum(gains, axis=0), "dp")
+    gain_all = lax.all_gather(call(fold_kernel, [((2 * HEADS, 128), F32)])(gains)[0], "dp")
     results = call(
         unpack_kernel,
         [((TOK, HEADS * KD), BF16)] * 3,

time: 113 us -> 113 us (level)
  blocking collectives: 40.2 us -> 70.7 us
  waiting for transfers between devices: 30.9 us -> 5.36 us
  starting transfers between devices: 23.9 us -> 19.9 us
  Pallas kernels: 16.1 us -> 14.7 us
    all_to_all x0 -> x1, blocking collectives: none -> 29 us  [shards(): lax.all_to_all(packed, 'ctx', 0, 0, axis_index_groups=halves, tiled=True)]
    all_to_all x2 -> x1, waiting for transfers between devices: 29.2 us -> 3.65 us  [shards(): lax.all_to_all(call(spread_kernel, [((blocks, 8, 128), F32)], cost=(4 * 1...]
    all_to_all x2 -> x1, starting transfers between devices: 9.75 us -> 3.5 us  [shards(): lax.all_to_all(call(spread_kernel, [((blocks, 8, 128), F32)], cost=(4 * 1...]
    ppermute x1, starting transfers between devices: 5.36 us -> 7.98 us  [shards(): middle = lax.ppermute(total, 'ctx', swap)]
    all_gather x1, blocking collectives: 40.2 us -> 41.7 us  [shards(): lax.all_gather(call(fold_kernel, [((2 * HEADS, 128), F32)])(gains)[0], 'dp')]
    pallas_call x7 -> x8, Pallas kernels: 16.1 us -> 14.7 us  [run(): pl.pallas_call(kernel, out_shape=[(pltpu.HBM if i in far else jax.ShapeDt...]
  transfers between devices with their start and end apart: 5 -> 4, of which waited for: 3 -> 2; matrix products, arithmetic and copies ran while one was open for 1% -> 1% of each run, Pallas kernels for 4% -> 4%
where the time goes in v7:
time: 113 us; the launch traced here: 112 us
  blocking collectives  70.7 us (63%)
  starting transfers between devices  19.9 us (18%)
  Pallas kernels  14.7 us (13%)
  waiting for transfers between devices  5.36 us (5%)
    all_gather x1, blocking collectives, shards(): lax.all_gather(call(fold_kernel, [((2 * HEADS, 128), F32)])(gains)[0], 'dp')  41.7 us
    all_to_all x1, blocking collectives, shards(): lax.all_to_all(packed, 'ctx', 0, 0, axis_index_groups=halves, tiled=True)  29 us
    pallas_call x8, Pallas kernels, run(): pl.pallas_call(kernel, out_shape=[(pltpu.HBM if i in far else jax.ShapeDt...  14.7 us
    ppermute x1, starting transfers between devices, shards(): middle = lax.ppermute(total, 'ctx', swap)  7.98 us
    ppermute x1, starting transfers between devices, shards(): middle_grad = lax.ppermute(total_grad, 'ctx', swap)  4.85 us
    all_to_all x1, waiting for transfers between devices, shards(): lax.all_to_all(call(spread_kernel, [((blocks, 8, 128), F32)], cost=(4 * 1...  3.65 us
    all_to_all x1, starting transfers between devices, shards(): lax.all_to_all(back, 'ctx', 0, 0, axis_index_groups=halves, tiled=True)  3.58 us
    all_to_all x1, starting transfers between devices, shards(): lax.all_to_all(call(spread_kernel, [((blocks, 8, 128), F32)], cost=(4 * 1...  3.5 us
  transfers between devices with their start and end apart: 4, of which 2 were waited for; matrix products, arithmetic and copies ran while one was open for 1% of the time, Pallas kernels for 4%

profile of v7, /device:TPU:1, one launch (start us, length us, event | category | flops | bytes accessed | tf_op | source)
XLA Modules:
  0.0 112.1 jit_solution(11206142625959558867)
XLA Ops:
  0.6 3.2 %shard_map.93 = bf16[8,528,256]{2,1,0:T(8,128)(2,1)} custom-call(bf16[128,2048]{1,0:T(8,128)(2,1)} %bitcast.13, bf16[128,2048]{1,0:T(8,128)(2,1)} %bitcast.14, bf16[128,2048]{1,0:T(8,128)(2,1)} %bitcast.15, bf16[128,2048]{1,0:T(8,128)(2,1)} %bitcast.16, f32[8,128]{1,0:T(8,128)} %bitcast.17), custom_call_target="tpu_custom_call" | custom-call | tf_op jit(solution)/shard_map/pallas_call | solution.py:44
  3.8 29.0 %all_to_all.15.got_ref = bf16[8,528,256]{2,1,0:T(8,128)(2,1)S(1)} all-to-all(bf16[8,528,256]{2,1,0:T(8,128)(2,1)} %shard_map.93), channel_id=1, replica_groups={{0,1,2,3,4,5,6,7},{8,9,10,11,12,13,14,15},{16,17,18,19,20,21,22,23},{24..., dimensions={0} | all-to-all | bytes 4325376 | tf_op jit(solution)/shard_map/all_to_all | solution.py:312
  32.8 0.0 copy-start
  32.8 1.6 %shard_map.94 = (bf16[256,256]{1,0:T(8,128)(2,1)}, f32[4,256,256]{2,1,0:T(8,128)S(1)}, f32[256,8]{1,0:T(8,128)S(1)}, f32[8,256]{1,0:T(8,128)S(1)}) custom-call(bf16[8,528,256]{2,1,0:T(8,128)(2,1)S(1)} %all_to_all.15.got_ref), custom_call_target="tpu_custom_call" | custom-call | tf_op jit(solution)/shard_map/pallas_call | solution.py:44
  34.4 8.0 %collective-permute-start = (bf16[256,256]{1,0:T(8,128)(2,1)}, bf16[256,256]{1,0:T(8,128)(2,1)S(1)}, u32[]{:S(2)}, u32[]{:S(2)}) collective-permute-start(bf16[256,256]{1,0:T(8,128)(2,1)} %get-tuple-element.21), channel_id=1, source_target_pairs={{0,8},{1,9},{2,10},{3,11},{4,12},{5,13},{6,14},{7,15},{8,0},{9,1},... | collective-permute-start | bytes 393224 | tf_op jit(solution)/shard_map/ppermute | solution.py:320
  42.4 0.0 copy-done
  42.5 0.8 shard_map.95
  43.3 1.7 %collective-permute-done.middle_ref = bf16[256,256]{1,0:T(8,128)(2,1)S(1)} collective-permute-done((bf16[256,256]{1,0:T(8,128)(2,1)}, bf16[256,256]{1,0:T(8,128)(2,1)S(1)}, u32[]{:S(2)}, u32[]{:S(2)}) %collective-permute-start) | collective-permute-done | bytes 131104 | tf_op jit(solution)/shard_map/ppermute | solution.py:320
  45.0 4.4 %shard_map.96 = (bf16[8,384,256]{2,1,0:T(8,128)(2,1)}, bf16[256,256]{1,0:T(8,128)(2,1)}, f32[8,128]{1,0:T(8,128)S(1)}) custom-call(s32[1]{0:T(128)} %bitcast.where_ref, bf16[8,528,256]{2,1,0:T(8,128)(2,1)S(1)} %all_to_all.15.got_ref, f32[4,256,256]{2,1,0:T(8,128)S(1)} %get-tuple-element.16.states_ref, ...), custom_call_target="tpu_custom_call" | custom-call | tf_op jit(solution)/shard_map/pallas_call | solution.py:44
  49.4 4.9 %collective-permute-start.1 = (bf16[256,256]{1,0:T(8,128)(2,1)}, bf16[256,256]{1,0:T(8,128)(2,1)S(1)}, u32[]{:S(2)}, u32[]{:S(2)}) collective-permute-start(bf16[256,256]{1,0:T(8,128)(2,1)} %get-tuple-element.23), channel_id=1, source_target_pairs={{0,8},{1,9},{2,10},{3,11},{4,12},{5,13},{6,14},{7,15},{8,0},{9,1},... | collective-permute-start | bytes 393224 | tf_op jit(solution)/shard_map/ppermute | solution.py:336
  54.3 0.6 shard_map.99
  54.9 3.5 %all-to-all-start.2 = ((f32[16,8,128]{2,1,0:T(8,128)}), f32[16,8,128]{2,1,0:T(8,128)S(1)}, u32[]{:S(2)}, u32[]{:S(2)}) async-start(f32[16,8,128]{2,1,0:T(8,128)} %shard_map.99), calls=%async_computation.2 | async-start | bytes 131072 | tf_op jit(solution)/shard_map/all_to_all | solution.py:337
  58.4 0.0 collective-permute-done.1.middle_ref
  58.4 2.8 %shard_map.97 = bf16[8,384,256]{2,1,0:T(8,128)(2,1)} custom-call(s32[1]{0:T(128)} %bitcast.where_ref, bf16[8,528,256]{2,1,0:T(8,128)(2,1)S(1)} %all_to_all.15.got_ref, bf16[8,384,256]{2,1,0:T(8,128)(2,1)} %get-tuple-element.22.back_ref, bf16[256,256]{1,0:T(8,128)(2,1)S(1)} %collective-permute-done.1.middle_ref, ...), custom_call_target="tpu_custom_call", output_to_operand_aliasing={{}: (2, {})} | custom-call | tf_op jit(solution)/shard_map/pallas_call | solution.py:44
  61.2 3.7 %all-to-all-done.2.gains_ref = f32[16,8,128]{2,1,0:T(8,128)S(1)} async-done(((f32[16,8,128]{2,1,0:T(8,128)}), f32[16,8,128]{2,1,0:T(8,128)S(1)}, u32[]{:S(2)}, u32[]{:S(2)}) %all-to-all-start.2) | async-done | bytes 65568 | tf_op jit(solution)/shard_map/all_to_all | solution.py:337
  64.9 3.6 %all-to-all-start.1 = ((bf16[8,384,256]{2,1,0:T(8,128)(2,1)}), bf16[8,384,256]{2,1,0:T(8,128)(2,1)S(1)}, u32[]{:S(2)}, u32[]{:S(2)}) async-start(bf16[8,384,256]{2,1,0:T(8,128)(2,1)} %shard_map.97), calls=%async_computation.1 | async-start | bytes 3145728 | tf_op jit(solution)/shard_map/all_to_all | solution.py:349
  68.5 41.7 %all-gather = f32[512,128]{1,0:T(8,128)S(1)} all-gather(f32[16,128]{1,0:T(8,128)S(1)} %shard_map.100), channel_id=2, replica_groups=mesh['dp'=32,'ctx'=16] {'dp'}, dimensions={0}, use_global_device_ids=true | all-gather | bytes 270336 | tf_op jit(solution)/shard_map/all_gather | solution.py:350
  110.2 0.6 multiply_bitcast_fusion
  110.8 0.0 all-to-all-done.1.got_ref
  110.8 1.3 %shard_map.98 = (bf16[128,2048]{1,0:T(8,128)(2,1)}, bf16[128,2048]{1,0:T(8,128)(2,1)}, bf16[128,2048]{1,0:T(8,128)(2,1)}) custom-call(bf16[8,384,256]{2,1,0:T(8,128)(2,1)S(1)} %all-to-all-done.1.got_ref), custom_call_target="tpu_custom_call" | custom-call | tf_op jit(solution)/shard_map/pallas_call | solution.py:44
  (4 shorter events, 0.1 us)
Async XLA Ops:
  32.8 9.6 %copy-start = (f32[2048]{0:T(1024)S(1)}, f32[2048]{0:T(1024)}, u32[]{:S(2)}) copy-start(f32[2048]{0:T(1024)} %param.11) | copy-start | bytes 24580
  34.4 10.5 %collective-permute-start = (bf16[256,256]{1,0:T(8,128)(2,1)}, bf16[256,256]{1,0:T(8,128)(2,1)S(1)}, u32[]{:S(2)}, u32[]{:S(2)}) collective-permute-start(bf16[256,256]{1,0:T(8,128)(2,1)} %get-tuple-element.21), channel_id=1, source_target_pairs={{0,8},{1,9},{2,10},{3,11},{4,12},{5,13},{6,14},{7,15},{8,0},{9,1},... | collective-permute-start | bytes 393224 | tf_op jit(solution)/shard_map/ppermute | solution.py:320
  49.4 9.0 %collective-permute-start.1 = (bf16[256,256]{1,0:T(8,128)(2,1)}, bf16[256,256]{1,0:T(8,128)(2,1)S(1)}, u32[]{:S(2)}, u32[]{:S(2)}) collective-permute-start(bf16[256,256]{1,0:T(8,128)(2,1)} %get-tuple-element.23), channel_id=1, source_target_pairs={{0,8},{1,9},{2,10},{3,11},{4,12},{5,13},{6,14},{7,15},{8,0},{9,1},... | collective-permute-start | bytes 393224 | tf_op jit(solution)/shard_map/ppermute | solution.py:336
  54.9 10.0 %all-to-all-start.2 = ((f32[16,8,128]{2,1,0:T(8,128)}), f32[16,8,128]{2,1,0:T(8,128)S(1)}, u32[]{:S(2)}, u32[]{:S(2)}) async-start(f32[16,8,128]{2,1,0:T(8,128)} %shard_map.99), calls=%async_computation.2 | async-start | bytes 131072 | tf_op jit(solution)/shard_map/all_to_all | solution.py:337
  64.9 46.0 %all-to-all-start.1 = ((bf16[8,384,256]{2,1,0:T(8,128)(2,1)}), bf16[8,384,256]{2,1,0:T(8,128)(2,1)S(1)}, u32[]{:S(2)}, u32[]{:S(2)}) async-start(bf16[8,384,256]{2,1,0:T(8,128)(2,1)} %shard_map.97), calls=%async_computation.1 | async-start | bytes 3145728 | tf_op jit(solution)/shard_map/all_to_all | solution.py:349

commit v8 on v7

--- a/solution.py
+++ b/solution.py
@@ -63,16 +63,14 @@
     return run
 
 
-def pack_kernel(
-    q_ref, k_ref, v_ref, g_ref, decay_ref, out_ref, buf, decay_buf, sems, decay_sem, out_sems
-):
+def pack_kernel(q_ref, k_ref, v_ref, g_ref, decay_ref, out_ref, decay_buf, sems, decay_sem):
     fetch = pltpu.make_async_copy(decay_ref, decay_buf, decay_sem)
     fetch.start()
     copies = [
         [
             pltpu.make_async_copy(
                 ref.at[:, h * KD : (h + 1) * KD],
-                buf.at[h, n * TOK : (n + 1) * TOK, :],
+                out_ref.at[h, n * TOK : (n + 1) * TOK, :],
                 sems.at[h, n],
             )
             for n, ref in enumerate((q_ref, k_ref, v_ref, g_ref))
@@ -92,15 +90,9 @@
         first = jnp.concatenate([high, middle], axis=1)
         second = jnp.concatenate([low, jnp.zeros_like(low)], axis=1)
         pieces = jnp.where(row == 0, first, jnp.where(row == 1, second, 0.0))
-        buf[h, 4 * TOK :, :] = pieces.astype(BF16)
-    stores = []
-    for h in range(HEADS):
-        for copy in copies[h]:
-            copy.wait()
-        stores.append(pltpu.make_async_copy(buf.at[h], out_ref.at[h], out_sems.at[h]))
-        stores[-1].start()
-    for store in stores:
-        store.wait()
+        out_ref[h, 4 * TOK :, :] = pieces.astype(BF16)
+    for copy in sum(copies, []):
+        copy.wait()
 
 
 def part(ref, c, n):
@@ -300,14 +292,11 @@
         pack_kernel,
         [((GROUP, ROWS, 256), BF16)],
         [
-            pltpu.VMEM((GROUP, ROWS, 256), BF16),
             pltpu.VMEM((HEADS, TOK), F32),
             pltpu.SemaphoreType.DMA((HEADS, 4)),
             pltpu.SemaphoreType.DMA,
-            pltpu.SemaphoreType.DMA((HEADS,)),
         ],
         places={i: pltpu.HBM for i in range(5)},
-        far=(0,),
     )(queries[0], key_vectors[0], values[0], grad_out[0], log_decay[0])[0]
     got = lax.all_to_all(packed, "ctx", 0, 0, axis_index_groups=halves, tiled=True)
     where = (place // GROUP).astype(jnp.int32).reshape(1)

time: 113 us -> 111 us (0.982)
  Pallas kernels: 14.7 us -> 13.4 us
    pallas_call x8, Pallas kernels: 14.7 us -> 13.4 us  [run(): pl.pallas_call(kernel, out_shape=[(pltpu.HBM if i in far else jax.ShapeDt...]
where the time goes in v8:
time: 111 us
  blocking collectives  71.4 us (64%)
  starting transfers between devices  19 us (17%)
  Pallas kernels  13.4 us (12%)
  waiting for transfers between devices  5.36 us (5%)
    all_gather x1, blocking collectives, shards(): lax.all_gather(call(fold_kernel, [((2 * HEADS, 128), F32)])(gains)[0], 'dp')  41.7 us
    all_to_all x1, blocking collectives, shards(): lax.all_to_all(packed, 'ctx', 0, 0, axis_index_groups=halves, tiled=True)  29.7 us
    pallas_call x8, Pallas kernels, run(): pl.pallas_call(kernel, out_shape=[(pltpu.HBM if i in far else jax.ShapeDt...  13.4 us
    ppermute x1, starting transfers between devices, shards(): middle = lax.ppermute(total, 'ctx', swap)  7.04 us
    ppermute x1, starting transfers between devices, shards(): middle_grad = lax.ppermute(total_grad, 'ctx', swap)  4.87 us
    all_to_all x1, waiting for transfers between devices, shards(): lax.all_to_all(call(spread_kernel, [((blocks, 8, 128), F32)], cost=(4 * 1...  3.65 us
    all_to_all x1, starting transfers between devices, shards(): lax.all_to_all(back, 'ctx', 0, 0, axis_index_groups=halves, tiled=True)  3.58 us
    all_to_all x1, starting transfers between devices, shards(): lax.all_to_all(call(spread_kernel, [((blocks, 8, 128), F32)], cost=(4 * 1...  3.5 us
  transfers between devices with their start and end apart: 4, of which 2 were waited for; matrix products, arithmetic and copies ran while one was open for 1% of the time, Pallas kernels for 4%

profile of v8, /device:TPU:1, one launch (start us, length us, event | category | flops | bytes accessed | tf_op | source)
XLA Modules:
  0.0 110.6 jit_solution(2581579982349801505)
XLA Ops:
  0.6 1.9 %shard_map.93 = bf16[8,528,256]{2,1,0:T(8,128)(2,1)S(1)} custom-call(bf16[128,2048]{1,0:T(8,128)(2,1)} %bitcast.13, bf16[128,2048]{1,0:T(8,128)(2,1)} %bitcast.14, bf16[128,2048]{1,0:T(8,128)(2,1)} %bitcast.15, bf16[128,2048]{1,0:T(8,128)(2,1)} %bitcast.16, f32[8,128]{1,0:T(8,128)} %bitcast.17), custom_call_target="tpu_custom_call" | custom-call | tf_op jit(solution)/shard_map/pallas_call | solution.py:44
  2.5 29.7 %all_to_all.15.got_ref = bf16[8,528,256]{2,1,0:T(8,128)(2,1)S(1)} all-to-all(bf16[8,528,256]{2,1,0:T(8,128)(2,1)S(1)} %shard_map.93), channel_id=1, replica_groups={{0,1,2,3,4,5,6,7},{8,9,10,11,12,13,14,15},{16,17,18,19,20,21,22,23},{24..., dimensions={0} | all-to-all | bytes 4325376 | tf_op jit(solution)/shard_map/all_to_all | solution.py:301
  32.3 0.0 copy-start
  32.3 1.6 %shard_map.94 = (bf16[256,256]{1,0:T(8,128)(2,1)}, f32[4,256,256]{2,1,0:T(8,128)S(1)}, f32[256,8]{1,0:T(8,128)S(1)}, f32[8,256]{1,0:T(8,128)S(1)}) custom-call(bf16[8,528,256]{2,1,0:T(8,128)(2,1)S(1)} %all_to_all.15.got_ref), custom_call_target="tpu_custom_call" | custom-call | tf_op jit(solution)/shard_map/pallas_call | solution.py:44
  33.9 7.0 %collective-permute-start = (bf16[256,256]{1,0:T(8,128)(2,1)}, bf16[256,256]{1,0:T(8,128)(2,1)S(1)}, u32[]{:S(2)}, u32[]{:S(2)}) collective-permute-start(bf16[256,256]{1,0:T(8,128)(2,1)} %get-tuple-element.21), channel_id=1, source_target_pairs={{0,8},{1,9},{2,10},{3,11},{4,12},{5,13},{6,14},{7,15},{8,0},{9,1},... | collective-permute-start | bytes 393224 | tf_op jit(solution)/shard_map/ppermute | solution.py:309
  40.9 0.0 copy-done
  41.0 0.8 shard_map.95
  41.8 1.7 %collective-permute-done.middle_ref = bf16[256,256]{1,0:T(8,128)(2,1)S(1)} collective-permute-done((bf16[256,256]{1,0:T(8,128)(2,1)}, bf16[256,256]{1,0:T(8,128)(2,1)S(1)}, u32[]{:S(2)}, u32[]{:S(2)}) %collective-permute-start) | collective-permute-done | bytes 131104 | tf_op jit(solution)/shard_map/ppermute | solution.py:309
  43.5 4.4 %shard_map.96 = (bf16[8,384,256]{2,1,0:T(8,128)(2,1)}, bf16[256,256]{1,0:T(8,128)(2,1)}, f32[8,128]{1,0:T(8,128)S(1)}) custom-call(s32[1]{0:T(128)} %bitcast.where_ref, bf16[8,528,256]{2,1,0:T(8,128)(2,1)S(1)} %all_to_all.15.got_ref, f32[4,256,256]{2,1,0:T(8,128)S(1)} %get-tuple-element.16.states_ref, ...), custom_call_target="tpu_custom_call" | custom-call | tf_op jit(solution)/shard_map/pallas_call | solution.py:44
  47.9 4.9 %collective-permute-start.1 = (bf16[256,256]{1,0:T(8,128)(2,1)}, bf16[256,256]{1,0:T(8,128)(2,1)S(1)}, u32[]{:S(2)}, u32[]{:S(2)}) collective-permute-start(bf16[256,256]{1,0:T(8,128)(2,1)} %get-tuple-element.23), channel_id=1, source_target_pairs={{0,8},{1,9},{2,10},{3,11},{4,12},{5,13},{6,14},{7,15},{8,0},{9,1},... | collective-permute-start | bytes 393224 | tf_op jit(solution)/shard_map/ppermute | solution.py:325
  52.8 0.6 shard_map.99
  53.4 3.5 %all-to-all-start.2 = ((f32[16,8,128]{2,1,0:T(8,128)}), f32[16,8,128]{2,1,0:T(8,128)S(1)}, u32[]{:S(2)}, u32[]{:S(2)}) async-start(f32[16,8,128]{2,1,0:T(8,128)} %shard_map.99), calls=%async_computation.2 | async-start | bytes 131072 | tf_op jit(solution)/shard_map/all_to_all | solution.py:326
  56.9 0.0 collective-permute-done.1.middle_ref
  56.9 2.8 %shard_map.97 = bf16[8,384,256]{2,1,0:T(8,128)(2,1)} custom-call(s32[1]{0:T(128)} %bitcast.where_ref, bf16[8,528,256]{2,1,0:T(8,128)(2,1)S(1)} %all_to_all.15.got_ref, bf16[8,384,256]{2,1,0:T(8,128)(2,1)} %get-tuple-element.22.back_ref, bf16[256,256]{1,0:T(8,128)(2,1)S(1)} %collective-permute-done.1.middle_ref, ...), custom_call_target="tpu_custom_call", output_to_operand_aliasing={{}: (2, {})} | custom-call | tf_op jit(solution)/shard_map/pallas_call | solution.py:44
  59.7 3.7 %all-to-all-done.2.gains_ref = f32[16,8,128]{2,1,0:T(8,128)S(1)} async-done(((f32[16,8,128]{2,1,0:T(8,128)}), f32[16,8,128]{2,1,0:T(8,128)S(1)}, u32[]{:S(2)}, u32[]{:S(2)}) %all-to-all-start.2) | async-done | bytes 65568 | tf_op jit(solution)/shard_map/all_to_all | solution.py:326
  63.4 3.6 %all-to-all-start.1 = ((bf16[8,384,256]{2,1,0:T(8,128)(2,1)}), bf16[8,384,256]{2,1,0:T(8,128)(2,1)S(1)}, u32[]{:S(2)}, u32[]{:S(2)}) async-start(bf16[8,384,256]{2,1,0:T(8,128)(2,1)} %shard_map.97), calls=%async_computation.1 | async-start | bytes 3145728 | tf_op jit(solution)/shard_map/all_to_all | solution.py:338
  67.0 41.7 %all-gather = f32[512,128]{1,0:T(8,128)S(1)} all-gather(f32[16,128]{1,0:T(8,128)S(1)} %shard_map.100), channel_id=2, replica_groups=mesh['dp'=32,'ctx'=16] {'dp'}, dimensions={0}, use_global_device_ids=true | all-gather | bytes 270336 | tf_op jit(solution)/shard_map/all_gather | solution.py:339
  108.7 0.6 multiply_bitcast_fusion
  109.3 0.0 all-to-all-done.1.got_ref
  109.3 1.3 %shard_map.98 = (bf16[128,2048]{1,0:T(8,128)(2,1)}, bf16[128,2048]{1,0:T(8,128)(2,1)}, bf16[128,2048]{1,0:T(8,128)(2,1)}) custom-call(bf16[8,384,256]{2,1,0:T(8,128)(2,1)S(1)} %all-to-all-done.1.got_ref), custom_call_target="tpu_custom_call" | custom-call | tf_op jit(solution)/shard_map/pallas_call | solution.py:44
  (4 shorter events, 0.1 us)
Async XLA Ops:
  32.3 8.7 %copy-start = (f32[2048]{0:T(1024)S(1)}, f32[2048]{0:T(1024)}, u32[]{:S(2)}) copy-start(f32[2048]{0:T(1024)} %param.11) | copy-start | bytes 24580
  33.9 9.6 %collective-permute-start = (bf16[256,256]{1,0:T(8,128)(2,1)}, bf16[256,256]{1,0:T(8,128)(2,1)S(1)}, u32[]{:S(2)}, u32[]{:S(2)}) collective-permute-start(bf16[256,256]{1,0:T(8,128)(2,1)} %get-tuple-element.21), channel_id=1, source_target_pairs={{0,8},{1,9},{2,10},{3,11},{4,12},{5,13},{6,14},{7,15},{8,0},{9,1},... | collective-permute-start | bytes 393224 | tf_op jit(solution)/shard_map/ppermute | solution.py:309
  47.9 9.0 %collective-permute-start.1 = (bf16[256,256]{1,0:T(8,128)(2,1)}, bf16[256,256]{1,0:T(8,128)(2,1)S(1)}, u32[]{:S(2)}, u32[]{:S(2)}) collective-permute-start(bf16[256,256]{1,0:T(8,128)(2,1)} %get-tuple-element.23), channel_id=1, source_target_pairs={{0,8},{1,9},{2,10},{3,11},{4,12},{5,13},{6,14},{7,15},{8,0},{9,1},... | collective-permute-start | bytes 393224 | tf_op jit(solution)/shard_map/ppermute | solution.py:325
  53.4 10.0 %all-to-all-start.2 = ((f32[16,8,128]{2,1,0:T(8,128)}), f32[16,8,128]{2,1,0:T(8,128)S(1)}, u32[]{:S(2)}, u32[]{:S(2)}) async-start(f32[16,8,128]{2,1,0:T(8,128)} %shard_map.99), calls=%async_computation.2 | async-start | bytes 131072 | tf_op jit(solution)/shard_map/all_to_all | solution.py:326
  63.4 46.0 %all-to-all-start.1 = ((bf16[8,384,256]{2,1,0:T(8,128)(2,1)}), bf16[8,384,256]{2,1,0:T(8,128)(2,1)S(1)}, u32[]{:S(2)}, u32[]{:S(2)}) async-start(bf16[8,384,256]{2,1,0:T(8,128)(2,1)} %shard_map.97), calls=%async_computation.1 | async-start | bytes 3145728 | tf_op jit(solution)/shard_map/all_to_all | solution.py:338

commit v9 on v8

--- a/solution.py
+++ b/solution.py
@@ -263,7 +263,7 @@
         copy.wait()
 
 
-def unpack_kernel(got_ref, queries_ref, keys_ref, values_ref, sems):
+def unpack_kernel(got_ref, gains_ref, queries_ref, keys_ref, values_ref, gain_ref, sems):
     copies = []
     for n, ref in enumerate((queries_ref, keys_ref, values_ref)):
         for h in range(HEADS):
@@ -276,6 +276,10 @@
             )
     for copy in copies:
         copy.start()
+    gain = gains_ref[0]
+    for i in range(1, gains_ref.shape[0]):
+        gain = gain + gains_ref[i]
+    gain_ref[...] = gain / gains_ref.shape[0]
     for copy in copies:
         copy.wait()
 
@@ -284,7 +288,6 @@
     place = lax.axis_index("ctx")
     blocks = lax.axis_size("ctx")
     halves = [list(range(GROUP)), list(range(GROUP, 2 * GROUP))]
-    size = lax.axis_size("dp")
     swap = [(i, i ^ GROUP) for i in range(blocks)]
     square = (CHUNKS, CHUNK, 256)
 
@@ -337,15 +340,14 @@
     )(where, got, back, middle_grad, column, line)[0]
     back = lax.all_to_all(back, "ctx", 0, 0, axis_index_groups=halves, tiled=True)
     gain_all = lax.all_gather(call(fold_kernel, [((2 * HEADS, 128), F32)])(gains)[0], "dp")
-    results = call(
+    *results, grad_gain = call(
         unpack_kernel,
-        [((TOK, HEADS * KD), BF16)] * 3,
+        [*[((TOK, HEADS * KD), BF16)] * 3, ((2 * HEADS, 128), F32)],
         [pltpu.SemaphoreType.DMA((3 * HEADS,))],
         places={0: pl.ANY},
         far=(0, 1, 2),
-    )(back)
-    grad_gain = (jnp.sum(gain_all, axis=0) / size).reshape(HEADS * VD)
-    return (*(item[None] for item in results), grad_gain)
+    )(back, gain_all)
+    return (*(item[None] for item in results), grad_gain.reshape(HEADS * VD))
 
 
 def solution(mesh):

time: 111 us -> 111 us (level)
  transfers between devices with their start and end apart: 4 -> 4, of which waited for: 2 -> 2; matrix products, arithmetic and copies ran while one was open for 1% -> 0% of each run, Pallas kernels for 4% -> 4%
where the time goes in v9:
time: 111 us
  blocking collectives  71.4 us (64%)
  starting transfers between devices  19 us (17%)
  Pallas kernels  14 us (13%)
  waiting for transfers between devices  5.36 us (5%)
    all_gather x1, blocking collectives, shards(): lax.all_gather(call(fold_kernel, [((2 * HEADS, 128), F32)])(gains)[0], 'dp')  41.7 us
    all_to_all x1, blocking collectives, shards(): lax.all_to_all(packed, 'ctx', 0, 0, axis_index_groups=halves, tiled=True)  29.7 us
    pallas_call x8, Pallas kernels, run(): pl.pallas_call(kernel, out_shape=[(pltpu.HBM if i in far else jax.ShapeDt...  14 us
    ppermute x1, starting transfers between devices, shards(): middle = lax.ppermute(total, 'ctx', swap)  7.04 us
    ppermute x1, starting transfers between devices, shards(): middle_grad = lax.ppermute(total_grad, 'ctx', swap)  4.87 us
    all_to_all x1, waiting for transfers between devices, shards(): lax.all_to_all(call(spread_kernel, [((blocks, 8, 128), F32)], cost=(4 * 1...  3.65 us
    all_to_all x1, starting transfers between devices, shards(): lax.all_to_all(back, 'ctx', 0, 0, axis_index_groups=halves, tiled=True)  3.58 us
    all_to_all x1, starting transfers between devices, shards(): lax.all_to_all(call(spread_kernel, [((blocks, 8, 128), F32)], cost=(4 * 1...  3.5 us
  transfers between devices with their start and end apart: 4, of which 2 were waited for; matrix products, arithmetic and copies ran while one was open for 0% of the time, Pallas kernels for 4%

profile of v9, /device:TPU:1, one launch (start us, length us, event | category | flops | bytes accessed | tf_op | source)
XLA Modules:
  0.0 110.6 jit_solution(4553470752176846498)
XLA Ops:
  0.6 1.9 %shard_map.93 = bf16[8,528,256]{2,1,0:T(8,128)(2,1)S(1)} custom-call(bf16[128,2048]{1,0:T(8,128)(2,1)} %bitcast.12, bf16[128,2048]{1,0:T(8,128)(2,1)} %bitcast.13, bf16[128,2048]{1,0:T(8,128)(2,1)} %bitcast.14, bf16[128,2048]{1,0:T(8,128)(2,1)} %bitcast.15, f32[8,128]{1,0:T(8,128)} %bitcast.16), custom_call_target="tpu_custom_call" | custom-call | tf_op jit(solution)/shard_map/pallas_call | solution.py:44
  2.5 29.7 %all_to_all.15.got_ref = bf16[8,528,256]{2,1,0:T(8,128)(2,1)S(1)} all-to-all(bf16[8,528,256]{2,1,0:T(8,128)(2,1)S(1)} %shard_map.93), channel_id=1, replica_groups={{0,1,2,3,4,5,6,7},{8,9,10,11,12,13,14,15},{16,17,18,19,20,21,22,23},{24..., dimensions={0} | all-to-all | bytes 4325376 | tf_op jit(solution)/shard_map/all_to_all | solution.py:304
  32.3 0.0 copy-start
  32.3 1.6 %shard_map.94 = (bf16[256,256]{1,0:T(8,128)(2,1)}, f32[4,256,256]{2,1,0:T(8,128)S(1)}, f32[256,8]{1,0:T(8,128)S(1)}, f32[8,256]{1,0:T(8,128)S(1)}) custom-call(bf16[8,528,256]{2,1,0:T(8,128)(2,1)S(1)} %all_to_all.15.got_ref), custom_call_target="tpu_custom_call" | custom-call | tf_op jit(solution)/shard_map/pallas_call | solution.py:44
  33.9 7.0 %collective-permute-start = (bf16[256,256]{1,0:T(8,128)(2,1)}, bf16[256,256]{1,0:T(8,128)(2,1)S(1)}, u32[]{:S(2)}, u32[]{:S(2)}) collective-permute-start(bf16[256,256]{1,0:T(8,128)(2,1)} %get-tuple-element.22), channel_id=1, source_target_pairs={{0,8},{1,9},{2,10},{3,11},{4,12},{5,13},{6,14},{7,15},{8,0},{9,1},... | collective-permute-start | bytes 393224 | tf_op jit(solution)/shard_map/ppermute | solution.py:312
  40.9 0.0 copy-done
  41.0 0.8 shard_map.95
  41.8 1.7 %collective-permute-done.middle_ref = bf16[256,256]{1,0:T(8,128)(2,1)S(1)} collective-permute-done((bf16[256,256]{1,0:T(8,128)(2,1)}, bf16[256,256]{1,0:T(8,128)(2,1)S(1)}, u32[]{:S(2)}, u32[]{:S(2)}) %collective-permute-start) | collective-permute-done | bytes 131104 | tf_op jit(solution)/shard_map/ppermute | solution.py:312
  43.5 4.4 %shard_map.96 = (bf16[8,384,256]{2,1,0:T(8,128)(2,1)}, bf16[256,256]{1,0:T(8,128)(2,1)}, f32[8,128]{1,0:T(8,128)S(1)}) custom-call(s32[1]{0:T(128)} %bitcast.where_ref, bf16[8,528,256]{2,1,0:T(8,128)(2,1)S(1)} %all_to_all.15.got_ref, f32[4,256,256]{2,1,0:T(8,128)S(1)} %get-tuple-element.17.states_ref, ...), custom_call_target="tpu_custom_call" | custom-call | tf_op jit(solution)/shard_map/pallas_call | solution.py:44
  47.9 4.9 %collective-permute-start.1 = (bf16[256,256]{1,0:T(8,128)(2,1)}, bf16[256,256]{1,0:T(8,128)(2,1)S(1)}, u32[]{:S(2)}, u32[]{:S(2)}) collective-permute-start(bf16[256,256]{1,0:T(8,128)(2,1)} %get-tuple-element.24), channel_id=1, source_target_pairs={{0,8},{1,9},{2,10},{3,11},{4,12},{5,13},{6,14},{7,15},{8,0},{9,1},... | collective-permute-start | bytes 393224 | tf_op jit(solution)/shard_map/ppermute | solution.py:328
  52.8 0.6 shard_map.98
  53.4 3.5 %all-to-all-start.2 = ((f32[16,8,128]{2,1,0:T(8,128)}), f32[16,8,128]{2,1,0:T(8,128)S(1)}, u32[]{:S(2)}, u32[]{:S(2)}) async-start(f32[16,8,128]{2,1,0:T(8,128)} %shard_map.98), calls=%async_computation.2 | async-start | bytes 131072 | tf_op jit(solution)/shard_map/all_to_all | solution.py:329
  56.9 0.0 collective-permute-done.1.middle_ref
  56.9 2.8 %shard_map.97 = bf16[8,384,256]{2,1,0:T(8,128)(2,1)} custom-call(s32[1]{0:T(128)} %bitcast.where_ref, bf16[8,528,256]{2,1,0:T(8,128)(2,1)S(1)} %all_to_all.15.got_ref, bf16[8,384,256]{2,1,0:T(8,128)(2,1)} %get-tuple-element.23.back_ref, bf16[256,256]{1,0:T(8,128)(2,1)S(1)} %collective-permute-done.1.middle_ref, ...), custom_call_target="tpu_custom_call", output_to_operand_aliasing={{}: (2, {})} | custom-call | tf_op jit(solution)/shard_map/pallas_call | solution.py:44
  59.7 3.7 %all-to-all-done.2.gains_ref = f32[16,8,128]{2,1,0:T(8,128)S(1)} async-done(((f32[16,8,128]{2,1,0:T(8,128)}), f32[16,8,128]{2,1,0:T(8,128)S(1)}, u32[]{:S(2)}, u32[]{:S(2)}) %all-to-all-start.2) | async-done | bytes 65568 | tf_op jit(solution)/shard_map/all_to_all | solution.py:329
  63.4 3.6 %all-to-all-start.1 = ((bf16[8,384,256]{2,1,0:T(8,128)(2,1)}), bf16[8,384,256]{2,1,0:T(8,128)(2,1)S(1)}, u32[]{:S(2)}, u32[]{:S(2)}) async-start(bf16[8,384,256]{2,1,0:T(8,128)(2,1)} %shard_map.97), calls=%async_computation.1 | async-start | bytes 3145728 | tf_op jit(solution)/shard_map/all_to_all | solution.py:341
  67.0 41.7 %all-gather = f32[512,128]{1,0:T(8,128)S(1)} all-gather(f32[16,128]{1,0:T(8,128)S(1)} %shard_map.99), channel_id=2, replica_groups=mesh['dp'=32,'ctx'=16] {'dp'}, dimensions={0}, use_global_device_ids=true | all-gather | bytes 270336 | tf_op jit(solution)/shard_map/all_gather | solution.py:342
  108.7 0.0 all-to-all-done.1.got_ref
  108.7 1.9 %shard_map.100 = (bf16[128,2048]{1,0:T(8,128)(2,1)}, bf16[128,2048]{1,0:T(8,128)(2,1)}, bf16[128,2048]{1,0:T(8,128)(2,1)}, f32[16,128]{1,0:T(8,128)}) custom-call(bf16[8,384,256]{2,1,0:T(8,128)(2,1)S(1)} %all-to-all-done.1.got_ref, f32[32,16,128]{2,1,0:T(8,128)S(1)} %bitcast.11), custom_call_target="tpu_custom_call" | custom-call | tf_op jit(solution)/shard_map/pallas_call | solution.py:44
  (3 shorter events, 0.0 us)
Async XLA Ops:
  32.3 8.7 %copy-start = (f32[2048]{0:T(1024)S(1)}, f32[2048]{0:T(1024)}, u32[]{:S(2)}) copy-start(f32[2048]{0:T(1024)} %param.11) | copy-start | bytes 24580
  33.9 9.6 %collective-permute-start = (bf16[256,256]{1,0:T(8,128)(2,1)}, bf16[256,256]{1,0:T(8,128)(2,1)S(1)}, u32[]{:S(2)}, u32[]{:S(2)}) collective-permute-start(bf16[256,256]{1,0:T(8,128)(2,1)} %get-tuple-element.22), channel_id=1, source_target_pairs={{0,8},{1,9},{2,10},{3,11},{4,12},{5,13},{6,14},{7,15},{8,0},{9,1},... | collective-permute-start | bytes 393224 | tf_op jit(solution)/shard_map/ppermute | solution.py:312
  47.9 9.0 %collective-permute-start.1 = (bf16[256,256]{1,0:T(8,128)(2,1)}, bf16[256,256]{1,0:T(8,128)(2,1)S(1)}, u32[]{:S(2)}, u32[]{:S(2)}) collective-permute-start(bf16[256,256]{1,0:T(8,128)(2,1)} %get-tuple-element.24), channel_id=1, source_target_pairs={{0,8},{1,9},{2,10},{3,11},{4,12},{5,13},{6,14},{7,15},{8,0},{9,1},... | collective-permute-start | bytes 393224 | tf_op jit(solution)/shard_map/ppermute | solution.py:328
  53.4 10.0 %all-to-all-start.2 = ((f32[16,8,128]{2,1,0:T(8,128)}), f32[16,8,128]{2,1,0:T(8,128)S(1)}, u32[]{:S(2)}, u32[]{:S(2)}) async-start(f32[16,8,128]{2,1,0:T(8,128)} %shard_map.98), calls=%async_computation.2 | async-start | bytes 131072 | tf_op jit(solution)/shard_map/all_to_all | solution.py:329
  63.4 45.3 %all-to-all-start.1 = ((bf16[8,384,256]{2,1,0:T(8,128)(2,1)}), bf16[8,384,256]{2,1,0:T(8,128)(2,1)S(1)}, u32[]{:S(2)}, u32[]{:S(2)}) async-start(bf16[8,384,256]{2,1,0:T(8,128)(2,1)} %shard_map.97), calls=%async_computation.1 | async-start | bytes 3145728 | tf_op jit(solution)/shard_map/all_to_all | solution.py:341
